TPU v7x, 256 devices: a whole 4x4x8 slice. The times are simulated.
256 devices in a mesh: dp: 16 (over z_lo, x, core), seq: 16 (over z_hi, y).
Axes of the slice: x: 4, y: 4, z: 8 (z_hi: 4, z_lo: 2; z = z_hi * 2 + z_lo), core: 2. Of those that a mesh axis runs over, the one named last changes fastest.
Arguments:
- features: bfloat16 [16, 2048, 1024], P('dp', 'seq'), may hold values from -11 to 11
- labels: int32 [16, 2048], P('dp', 'seq'), may hold values from 0 to 172
- label_table: bfloat16 [173, 1024], replicated, may hold values from -3 to 3
- proj_weight: bfloat16 [1024, 4, 1024], P('seq'), may hold values from -0.1875 to 0.1875
- block_order: int32 [16, 16], P('dp'), may hold values from 0 to 15, as said below
- neighbours: int32 [16, 16, 4], P('dp'), may hold values from 0 to 15, as said below
- counts: int32 [16, 16], P('dp'), may hold values from 1 to 4, as said below
- cotangent: bfloat16 [16, 2048, 1024], P('dp', 'seq'), may hold values from -6 to 6
Outputs:
- layer_out: bfloat16 [16, 2048, 1024], P('dp', 'seq')
- features_grad: bfloat16 [16, 2048, 1024], P('dp', 'seq')
- proj_grad: float32 [1024, 4, 1024], P('seq')
Inputs may be any that keep to these rules, and one draw needn't show every extreme that they name: `block_order`: each subgraph's row is a permutation of the cluster ids. `neighbours`: slot 0 of stored block s names block_order[s] itself; slot j names block_order[s] + j * t modulo 16 for an odd step t of the row. `counts`: stored block 0 of every subgraph uses all 4 slots.
All inputs are finite; a program needn't handle non-finite values.
Results may differ from a plain program's by a relative error of at most 0.025.
Values may be sent and summed in bfloat16 or wider, within the bound.
A program may use at most 128 MiB of HBM per device.

v0:
```python
import math

import jax
import jax.numpy as jnp
from jax import lax
from jax.sharding import PartitionSpec as P

HEAD_DIM = 64


def slot_tables(order, neigh, cnt):
    blocks = order.shape[0]
    positions = lax.iota(jnp.int32, blocks)
    slot_of = jnp.sum(
        jnp.where(order[None, :] == positions[:, None], positions[None, :], 0), axis=1
    )
    key_slots = jnp.sum(
        jnp.where(neigh[:, :, None] == positions[None, None, :], slot_of[None, None, :], 0), axis=2
    )
    valid = lax.iota(jnp.int32, neigh.shape[1])[None, :] < cnt[:, None]
    return (key_slots, valid)


def block_probs(query, keys, live_slots, scale):
    scores = (
        jnp.einsum("gqhe,gjkhe->ghqjk", query, keys, preferred_element_type=jnp.float32) * scale
    )
    live = live_slots[:, None, None, :, None]
    top = jnp.max(jnp.where(live, scores, -1e30), axis=(3, 4), keepdims=True)
    expo = jnp.where(live, jnp.exp(scores - top), 0.0)
    return expo / jnp.sum(expo, axis=(3, 4), keepdims=True)


def layout(query, key_slots):
    nodes, heads, depth = query.shape
    blocks, neigh = key_slots.shape
    block = nodes // blocks
    group = math.gcd(blocks, max(1, 512 // block))
    return (nodes, heads, depth, blocks, neigh, block, group, blocks // group)


def attend(query, keyset, valueset, key_slots, valid):
    nodes, heads, depth, blocks, neigh, block, group, steps = layout(query, key_slots)
    scale = 1.0 / math.sqrt(depth)
    key_blocks = keyset.reshape(blocks, block, heads, depth)
    value_blocks = valueset.reshape(blocks, block, heads, depth)

    def one_step(pieces):
        rows, slots, live = pieces
        probs = block_probs(rows, key_blocks[slots], live, scale).astype(jnp.bfloat16)
        return jnp.einsum(
            "ghqjk,gjkhe->gqhe", probs, value_blocks[slots], preferred_element_type=jnp.float32
        ).astype(jnp.bfloat16)

    result = lax.map(
        one_step,
        (
            query.reshape(steps, group, block, heads, depth),
            key_slots.reshape(steps, group, neigh),
            valid.reshape(steps, group, neigh),
        ),
    )
    return result.reshape(nodes, heads * depth)


def attend_back(query, keyset, valueset, grad_out, key_slots, valid):
    nodes, heads, depth, blocks, neigh, block, group, steps = layout(query, key_slots)
    scale = 1.0 / math.sqrt(depth)
    key_blocks = keyset.reshape(blocks, block, heads, depth)
    value_blocks = valueset.reshape(blocks, block, heads, depth)
    positions = lax.iota(jnp.int32, blocks)

    def one_step(carry, pieces):
        key_acc, value_acc = carry
        rows, grad_rows, slots, live = pieces
        keys = key_blocks[slots]
        vals = value_blocks[slots]
        probs = block_probs(rows, keys, live, scale)
        probs_low = probs.astype(jnp.bfloat16)
        grad_p = jnp.einsum(
            "gqhe,gjkhe->ghqjk", grad_rows, vals, preferred_element_type=jnp.float32
        )
        delta = jnp.sum(probs * grad_p, axis=(3, 4), keepdims=True)
        grad_s = (probs * (grad_p - delta) * scale).astype(jnp.bfloat16)
        grad_q = jnp.einsum(
            "ghqjk,gjkhe->gqhe", grad_s, keys, preferred_element_type=jnp.float32
        ).astype(jnp.bfloat16)
        key_part = jnp.einsum("ghqjk,gqhe->gjkhe", grad_s, rows, preferred_element_type=jnp.float32)
        value_part = jnp.einsum(
            "ghqjk,gqhe->gjkhe", probs_low, grad_rows, preferred_element_type=jnp.float32
        )
        select = (slots.reshape(-1)[:, None] == positions[None, :]).astype(jnp.float32)
        key_acc = key_acc + jnp.einsum(
            "ib,ikhe->bkhe",
            select,
            key_part.reshape(group * neigh, block, heads, depth),
            precision=lax.Precision.HIGHEST,
        )
        value_acc = value_acc + jnp.einsum(
            "ib,ikhe->bkhe",
            select,
            value_part.reshape(group * neigh, block, heads, depth),
            precision=lax.Precision.HIGHEST,
        )
        return ((key_acc, value_acc), grad_q)

    empty = jnp.zeros((blocks, block, heads, depth), jnp.float32)
    pieces = (
        query.reshape(steps, group, block, heads, depth),
        grad_out.reshape(steps, group, block, heads, depth),
        key_slots.reshape(steps, group, neigh),
        valid.reshape(steps, group, neigh),
    )
    sums, grad_q = lax.scan(one_step, (empty, empty), pieces)
    grad_k = sums[0].astype(jnp.bfloat16).reshape(nodes, heads * depth)
    grad_v = sums[1].astype(jnp.bfloat16).reshape(nodes, heads * depth)
    return jnp.stack([grad_q.reshape(nodes, heads * depth), grad_k, grad_v], axis=1)


def per_device(
    features, labels, label_table, proj_weight, block_order, neighbours, counts, cotangent
):
    feat = features[0]
    cot = cotangent[0]
    node_dev, width = feat.shape
    rows = proj_weight.shape[0]
    onehot = (labels[0][:, None] == lax.iota(jnp.int32, label_table.shape[0])[None, :]).astype(
        jnp.bfloat16
    )
    hidden = (
        feat.astype(jnp.float32) + jnp.dot(onehot, label_table, preferred_element_type=jnp.float32)
    ).astype(jnp.bfloat16)
    weights = lax.all_gather(proj_weight, "seq", axis=0, tiled=True)
    in_proj = weights[:, :3].reshape(width, 3 * width)
    out_proj = weights[:, 3]
    qkv = (
        jnp.dot(hidden, in_proj, preferred_element_type=jnp.float32)
        .astype(jnp.bfloat16)
        .reshape(node_dev, 3, width)
    )
    head_qkv = lax.all_to_all(qkv, "seq", split_axis=2, concat_axis=0, tiled=True)
    nodes = head_qkv.shape[0]
    heads_here = rows // HEAD_DIM
    split = head_qkv.reshape(nodes, 3, heads_here, HEAD_DIM)
    query, keyset, valueset = (split[:, 0], split[:, 1], split[:, 2])
    key_slots, valid = slot_tables(block_order[0], neighbours[0], counts[0])
    attended = attend(query, keyset, valueset, key_slots, valid)
    attn = lax.all_to_all(attended, "seq", split_axis=0, concat_axis=1, tiled=True)
    layer_out = (
        hidden.astype(jnp.float32) + jnp.dot(attn, out_proj, preferred_element_type=jnp.float32)
    ).astype(jnp.bfloat16)
    weights_back = lax.all_gather(proj_weight, "seq", axis=0, tiled=True)
    in_back = weights_back[:, :3].reshape(width, 3 * width)
    out_back = weights_back[:, 3]
    contract_last = (((1,), (1,)), ((), ()))
    contract_first = (((0,), (0,)), ((), ()))
    grad_attn = lax.dot_general(
        cot, out_back, contract_last, preferred_element_type=jnp.float32
    ).astype(jnp.bfloat16)
    head_grad = lax.all_to_all(grad_attn, "seq", split_axis=1, concat_axis=0, tiled=True).reshape(
        nodes, heads_here, HEAD_DIM
    )
    stacked = attend_back(query, keyset, valueset, head_grad, key_slots, valid)
    grad_qkv = lax.all_to_all(stacked, "seq", split_axis=0, concat_axis=2, tiled=True).reshape(
        node_dev, 3 * width
    )
    features_grad = (
        lax.dot_general(grad_qkv, in_back, contract_last, preferred_element_type=jnp.float32)
        + cot.astype(jnp.float32)
    ).astype(jnp.bfloat16)
    proj_grad = lax.psum(
        lax.psum_scatter(
            jnp.concatenate(
                [
                    lax.dot_general(
                        hidden, grad_qkv, contract_first, preferred_element_type=jnp.float32
                    ).reshape(rows * lax.axis_size("seq"), 3, width),
                    lax.dot_general(attn, cot, contract_first, preferred_element_type=jnp.float32)[
                        :, None, :
                    ],
                ],
                axis=1,
            ).astype(jnp.bfloat16),
            "seq",
            scatter_dimension=0,
            tiled=True,
        ),
        "dp",
    ).astype(jnp.float32)
    return (layer_out[None], features_grad[None], proj_grad)


def solution(mesh):
    placed = (
        P("dp", "seq", None),
        P("dp", "seq"),
        P(),
        P("seq", None, None),
        P("dp", None),
        P("dp", None, None),
        P("dp", None),
        P("dp", "seq", None),
    )
    return jax.shard_map(
        per_device,
        mesh=mesh,
        in_specs=placed,
        out_specs=(P("dp", "seq", None), P("dp", "seq", None), P("seq", None, None)),
        check_vma=False,
    )
```

profile of v0, /device:TPU:1, one launch (start us, length us, event | category | flops | bytes accessed | tf_op | source)
XLA Modules:
  0.0 552.8 jit_solution(12046743255352382077)
XLA Ops:
  9.4 115.8 %all-gather.2.cloned.1.call-done = bf16[1024,4,1024]{2,1,0:T(4,128)(2,1)} async-done(((bf16[64,4,1024]{2,1,0:T(4,128)(2,1)}), bf16[1024,4,1024]{2,1,0:T(4,128)(2,1)}) %all-gather.2.cloned.1.call-update) | async-done | bytes 8388624 | tf_op jit(solution)/shard_map/all_gather | solution.py:133
  125.2 13.0 %copy.148 = bf16[1024,3,1024]{0,2,1:T(8,128)(2,1)} copy(bf16[1024,3,1024]{2,1,0:T(4,128)(2,1)} %bitcast.282) | data formatting | bytes 12582912
  138.3 5.0 convolution_convert_fusion
  145.3 12.0 %all-to-all-start = ((bf16[128,3,1024]{0,1,2:T(4,128)(2,1)}), bf16[128,3,1024]{0,1,2:T(4,128)(2,1)S(1)}, u32[]{:S(2)}, u32[]{:S(2)}) async-start(bf16[128,3,1024]{0,1,2:T(4,128)(2,1)} %copy.115), calls=%async_computation | async-start | bytes 2097152 | tf_op jit(solution)/shard_map/all_to_all | solution.py:141
  159.3 10.0 %slice.34 = bf16[1024,1,1024]{2,1,0:T(2,128)(2,1)} slice(bf16[1024,4,1024]{2,1,0:T(4,128)(2,1)} %all-gather.2.cloned.1.call-done), slice={[0:1024], [3:4], [0:1024]} | slice | bytes 4194304 | tf_op jit(solution)/shard_map/slice | solution.py:135
  169.3 3.1 convolution_convert_fusion.2
  173.2 9.9 %all-to-all-done = bf16[128,3,1024]{0,1,2:T(4,128)(2,1)S(1)} async-done(((bf16[128,3,1024]{0,1,2:T(4,128)(2,1)}), bf16[128,3,1024]{0,1,2:T(4,128)(2,1)S(1)}, u32[]{:S(2)}, u32[]{:S(2)}) %all-to-all-start) | async-done | bytes 786464 | tf_op jit(solution)/shard_map/all_to_all | solution.py:141
  183.1 7.6 %all-to-all-start.2 = ((bf16[128,16,64]{0,2,1:T(8,128)(2,1)}), bf16[128,16,64]{0,2,1:T(8,128)(2,1)}, u32[]{:S(2)}, u32[]{:S(2)}) async-start(bf16[128,16,64]{0,2,1:T(8,128)(2,1)} %bitcast.28), calls=%async_computation.2 | async-start | bytes 524288 | tf_op jit(solution)/shard_map/all_to_all | solution.py:160
  192.3 12.0 %while.25 = (s32[]{:T(128)}, bf16[4,4,128,1,64]{2,4,1,3,0:T(8,128)(2,1)}, s32[4,4,4]{2,1,0:T(4,128)S(1)}, bf16[16,128,1,64]{1,3,2,0:T(8,128)(2,1)S(1)}, pred[4,4...) while((s32[]{:T(128)}, ...), condition=%wide.region_5.6_spmd, body=%wide.region_2.5_spmd.sunk | while | flops 69763120 | bytes 4865133 | solution.py:55
  204.3 9.0 %all-to-all-start.1 = ((bf16[16,128,64]{1,2,0:T(8,128)(2,1)}), bf16[16,128,64]{1,2,0:T(8,128)(2,1)}, u32[]{:S(2)}, u32[]{:S(2)}) async-start(bf16[16,128,64]{1,2,0:T(8,128)(2,1)} %bitcast.22), calls=%async_computation.1 | async-start | bytes 524288 | tf_op jit(solution)/shard_map/all_to_all | solution.py:148
  213.3 37.3 %while.26 = (s32[]{:T(128)}, f32[16,128,1,64]{1,0,3,2:T(8,128)}, f32[16,128,1,64]{1,0,3,2:T(8,128)}, bf16[4,4,128,1,64]{2,1,0,4,3:T(4,128)(2,1)}, s32[4,4,4]{2,1...) while((s32[]{:T(128)}, f32[16,128,1,64]{1,0,3,2:T(8,128)}, ...), condition=%wide.region_10.11_spmd.clone, body=%wide.region_6.10_spmd.clone.sunk | while | flops 224428080 | bytes 19623484 | solution.py:114
  225.9 2.6 fusion.105
  235.5 2.6 fusion.105
  245.1 2.6 fusion.105
  255.7 2.5 reshape.309
  258.2 9.0 %all-to-all-start.3 = ((bf16[16,2,12288]{2,1,0:T(2,128)(2,1)}), bf16[16,2,12288]{2,1,0:T(2,128)(2,1)S(1)}, u32[]{:S(2)}, u32[]{:S(2)}) async-start(bf16[16,2,12288]{2,1,0:T(2,128)(2,1)} %reshape.309), calls=%async_computation.3 | async-start | bytes 1572864 | tf_op jit(solution)/shard_map/all_to_all | solution.py:164
  267.2 3.0 convert_bitcast_fusion
  270.2 18.8 %all-to-all-done.3 = bf16[16,2,12288]{2,1,0:T(2,128)(2,1)S(1)} async-done(((bf16[16,2,12288]{2,1,0:T(2,128)(2,1)}), bf16[16,2,12288]{2,1,0:T(2,128)(2,1)S(1)}, u32[]{:S(2)}, u32[]{:S(2)}) %all-to-all-start.3) | async-done | bytes 786464 | tf_op jit(solution)/shard_map/all_to_all | solution.py:164
  292.4 3.0 convolution_convert_fusion.1
  295.5 5.5 %pad_maximum_fusion = bf16[1024,4,1024]{2,0,1:T(8,128)(2,1)} fusion(bf16[1024,1,1024]{2,0,1:T(8,128)(2,1)} %convert_bitcast_fusion, bf16[1024,3,1024]{2,0,1:T(8,128)(2,1)S(1)} %convolution_convert_fusion.1), kind=kLoop, calls=%fused_computation.63 | loop fusion | flops 4194304 | bytes 16777216 | tf_op jit(solution)/shard_map/concatenate | solution.py:173
  301.1 119.1 %reduce-scatter.2.cloned.1.call-done = bf16[64,4,1024]{2,0,1:T(8,128)(2,1)} async-done(((bf16[1024,4,1024]{2,0,1:T(8,128)(2,1)}), bf16[64,4,1024]{2,0,1:T(8,128)(2,1)}) %reduce-scatter.2.cloned.1.call-update) | async-done | bytes 524304 | tf_op jit(solution)/shard_map/reduce_scatter | solution.py:172
  420.2 3.8 fusion.44
  424.1 4.5 fusion.45
  428.6 115.3 %all-reduce.2.cloned.1.call-done = bf16[64,4,1024]{2,0,1:T(8,128)(2,1)} async-done(((bf16[64,4,1024]{2,0,1:T(8,128)(2,1)}), bf16[64,4,1024]{2,0,1:T(8,128)(2,1)}) %all-reduce.2.cloned.1.call-update) | async-done | bytes 524304 | tf_op jit(solution)/shard_map/psum | solution.py:171
  (180 shorter events, 60.6 us)
Async XLA Ops:
  7.2 1.0 copy-start
  7.2 118.1 %all-gather.2.cloned.1.call-start = ((), (), s32[]{:S(2)}) async-start(), calls=%async_computation.5 | async-start | bytes 8912896 | tf_op jit(solution)/shard_map/all_gather | solution.py:133
  9.4 128.9 %copy-start.4 = (bf16[128,1024]{1,0:T(8,128)(2,1)}, bf16[128,1024]{1,0:T(8,128)(2,1)S(1)}, u32[]{:S(2)}) copy-start(bf16[128,1024]{1,0:T(8,128)(2,1)S(1)} %fusion.42) | copy-start | bytes 786436
  138.3 19.1 %copy-start.10 = (s32[1,16]{1,0:T(1,128)S(1)}, s32[1,16]{1,0:T(1,128)}, u32[]{:S(2)}) copy-start(s32[1,16]{1,0:T(1,128)} %param.16) | copy-start | bytes 196
  138.3 19.2 %copy-start.9 = (s32[1,16,4]{1,2,0:T(4,128)S(1)}, s32[1,16,4]{1,2,0:T(4,128)}, u32[]{:S(2)}) copy-start(s32[1,16,4]{1,2,0:T(4,128)} %param.17) | copy-start | bytes 772
  138.3 20.1 %copy-start.11 = (s32[1,16]{1,0:T(1,128)S(1)}, s32[1,16]{1,0:T(1,128)}, u32[]{:S(2)}) copy-start(s32[1,16]{1,0:T(1,128)} %param.18) | copy-start | bytes 196
  143.7 25.6 %copy-start.6 = (bf16[1,128,1024]{2,1,0:T(8,128)(2,1)S(1)}, bf16[1,128,1024]{2,1,0:T(8,128)(2,1)}, u32[]{:S(2)}) copy-start(bf16[1,128,1024]{2,1,0:T(8,128)(2,1)} %param.19) | copy-start | bytes 786436
  145.3 37.8 %all-to-all-start = ((bf16[128,3,1024]{0,1,2:T(4,128)(2,1)}), bf16[128,3,1024]{0,1,2:T(4,128)(2,1)S(1)}, u32[]{:S(2)}, u32[]{:S(2)}) async-start(bf16[128,3,1024]{0,1,2:T(4,128)(2,1)} %copy.115), calls=%async_computation | async-start | bytes 2097152 | tf_op jit(solution)/shard_map/all_to_all | solution.py:141
  183.1 21.2 %all-to-all-start.2 = ((bf16[128,16,64]{0,2,1:T(8,128)(2,1)}), bf16[128,16,64]{0,2,1:T(8,128)(2,1)}, u32[]{:S(2)}, u32[]{:S(2)}) async-start(bf16[128,16,64]{0,2,1:T(8,128)(2,1)} %bitcast.28), calls=%async_computation.2 | async-start | bytes 524288 | tf_op jit(solution)/shard_map/all_to_all | solution.py:160
  204.3 53.9 %all-to-all-start.1 = ((bf16[16,128,64]{1,2,0:T(8,128)(2,1)}), bf16[16,128,64]{1,2,0:T(8,128)(2,1)}, u32[]{:S(2)}, u32[]{:S(2)}) async-start(bf16[16,128,64]{1,2,0:T(8,128)(2,1)} %bitcast.22), calls=%async_computation.1 | async-start | bytes 524288 | tf_op jit(solution)/shard_map/all_to_all | solution.py:148
  217.4 2.7 copy-start.1
  220.9 0.9 copy-start.2
  225.9 3.8 copy-start.1
  230.5 0.9 copy-start.2
  235.5 3.8 copy-start.1
  245.1 3.8 copy-start.1
  249.7 0.9 copy-start.2
  250.6 16.6 %copy-start.7 = (bf16[1,128,1024]{2,1,0:T(8,128)(2,1)S(1)}, bf16[1,128,1024]{2,1,0:T(8,128)(2,1)}, u32[]{:S(2)}) copy-start(bf16[1,128,1024]{2,1,0:T(8,128)(2,1)} %param.19) | copy-start | bytes 786436
  258.2 30.8 %all-to-all-start.3 = ((bf16[16,2,12288]{2,1,0:T(2,128)(2,1)}), bf16[16,2,12288]{2,1,0:T(2,128)(2,1)S(1)}, u32[]{:S(2)}, u32[]{:S(2)}) async-start(bf16[16,2,12288]{2,1,0:T(2,128)(2,1)} %reshape.309), calls=%async_computation.3 | async-start | bytes 1572864 | tf_op jit(solution)/shard_map/all_to_all | solution.py:164
  267.2 153.0 %reduce-scatter.2.cloned.1.call-start = ((), (), s32[]{:S(2)}) async-start(), calls=%async_computation.6 | async-start | bytes 8912896 | tf_op jit(solution)/shard_map/reduce_scatter | solution.py:172
  301.0 119.2 %copy-start.5 = (bf16[128,1024]{1,0:T(8,128)(2,1)S(1)}, bf16[128,1024]{1,0:T(8,128)(2,1)}, u32[]{:S(2)}) copy-start(bf16[128,1024]{1,0:T(8,128)(2,1)} %copy-done.4) | copy-start | bytes 786436
  301.0 123.0 %copy-start.3 = (bf16[128,3,16,64]{0,3,2,1:T(8,128)(2,1)S(1)}, bf16[128,3,16,64]{0,3,2,1:T(8,128)(2,1)}, u32[]{:S(2)}) copy-start(bf16[128,3,16,64]{0,3,2,1:T(8,128)(2,1)} %copy.131) | copy-start | bytes 2359300
  301.0 123.0 %copy-start.8 = (bf16[1,128,1024]{2,1,0:T(8,128)(2,1)S(1)}, bf16[1,128,1024]{2,1,0:T(8,128)(2,1)}, u32[]{:S(2)}) copy-start(bf16[1,128,1024]{2,1,0:T(8,128)(2,1)} %param.19) | copy-start | bytes 786436
  301.0 242.8 %all-reduce.2.cloned.1.call-start = ((), (), s32[]{:S(2)}) async-start(), calls=%async_computation.7 | async-start | bytes 1048576 | tf_op jit(solution)/shard_map/psum | solution.py:171
  (1 other events, 0.9 us)
Sparse Core Ops, SparseCore 0:
  10.4 114.7 all-gather.1
  301.2 118.9 reduce-scatter.1
  422.8 120.9 all-reduce.1
where the time goes:
time: 554 us; the launch traced here: 553 us
  waiting for transfers between devices  380 us (69%)
  matrix products  55.4 us (10%)
  local copies, waits for them, and re-layouts  53 us (10%)
  starting transfers between devices  37.8 us (7%)
  between operations  14 us (3%)
  other arithmetic  12.6 us (2%)
    reduce_scatter x1, waiting for transfers between devices, per_device(): lax.psum_scatter(jnp.concatenate([lax.dot_general(hidden, grad_qkv, contr...  119 us
    all_gather x1, waiting for transfers between devices, per_device(): weights = lax.all_gather(proj_weight, 'seq', axis=0, tiled=True)  116 us
    psum x1, waiting for transfers between devices, per_device(): lax.psum(lax.psum_scatter(jnp.concatenate([lax.dot_general(hidden, grad_q...  115 us
    unnamed x28, local copies, waits for them, and re-layouts  20.2 us
    all_to_all x1, waiting for transfers between devices, per_device(): lax.all_to_all(stacked, 'seq', split_axis=0, concat_axis=2, tiled=True)  18.8 us
    all_to_all x1, starting transfers between devices, per_device(): lax.all_to_all(qkv, 'seq', split_axis=2, concat_axis=0, tiled=True)  12 us
  transfers between devices with their start and end apart: 7, of which 5 were waited for; matrix products, arithmetic and copies ran while one was open for 16% of the time, Pallas kernels for 0%

commit v1 on v0

v1 whole, which is shorter than its diff:
```python
import jax
import jax.numpy as jnp
from jax import lax
from jax.experimental import pallas as pl
from jax.experimental.pallas import tpu as pltpu
from jax.sharding import PartitionSpec as P

XS, YS, TEAM, SEQ, ROWS, WIDTH = 4, 4, 8, 16, 128, 1024
SHARD = WIDTH // SEQ
BF, F32 = jnp.bfloat16, jnp.float32
NN = (((1,), (0,)), ((), ()))
NT = (((1,), (1,)), ((), ()))
TN = (((0,), (0,)), ((), ()))
VMEM_BYTES = 48 << 20


def dot(a, b, dims=NN):
    return lax.dot_general(a, b, dims, preferred_element_type=F32)


def place():
    dp, seq = lax.axis_index("dp"), lax.axis_index("seq")
    return dp // TEAM, dp % TEAM, seq


def push(src, dst, send, recv, dp, seq):
    copy = pltpu.make_async_remote_copy(
        src_ref=src,
        dst_ref=dst,
        send_sem=send,
        recv_sem=recv,
        device_id=(dp, seq),
        device_id_type=pl.DeviceIdType.MESH,
    )
    copy.start()
    return copy


def await_recv(dst, recv, dp, seq):
    pltpu.make_async_remote_copy(
        src_ref=dst,
        dst_ref=dst,
        send_sem=recv,
        recv_sem=recv,
        device_id=(dp, seq),
        device_id_type=pl.DeviceIdType.MESH,
    ).wait_recv()


def greet(peers):
    barrier = pltpu.get_barrier_semaphore()
    for dp, seq in peers:
        pl.semaphore_signal(
            barrier, inc=1, device_id=(dp, seq), device_id_type=pl.DeviceIdType.MESH
        )
    pl.semaphore_wait(barrier, len(peers))


def low_lanes(shape):
    return lax.broadcasted_iota(jnp.int32, shape, 1) < 64


def merge(a, b):
    return jnp.where(low_lanes(a.shape), a, pltpu.roll(b, 64, 1))


def merge_high(a, b):
    return jnp.where(low_lanes(a.shape), pltpu.roll(a, 64, 1), b)


def gather_kernel(
    hid, cot, wt, tab,
    qg_out, hid8_out, cot8_out, wg_out, tab_out,
    hid8, cot8, wg, wo, tab8, vals, stage, land,
    hid_s, hid_r, cot_s, cot_r, tab_s, tab_r, w_s, w_r, o_s, o_r, sc_s, sc_r, a_s, a_r, loc,
):
    zl, p, r = place()
    x, c = p // 2, p % 2
    zh, y = r // YS, r % YS
    base = zl * TEAM
    dp = base + p

    def team(dx, dc):
        return lax.rem(x + dx, XS) * 2 + lax.rem(c + dc, 2)

    def at_z(k):
        return lax.rem(zh + k, 4) * YS + y

    def at_y(k):
        return zh * YS + lax.rem(y + k, YS)

    greet(
        [(base + lax.rem(p + k, TEAM), r) for k in range(1, TEAM)]
        + [(dp, lax.rem(r + k, SEQ)) for k in range(1, SEQ)]
    )
    sends = []

    def rows_of(s):
        return pl.ds(pl.multiple_of(s * SHARD, SHARD), SHARD)

    def in_part(s):
        return wg.at[rows_of(s), 0:384]

    def out_part(s):
        return wg.at[rows_of(s), 384:512]

    own = pltpu.make_async_copy(wt.at[p, :, 0:384], in_part(r), loc.at[0])
    own.start()
    for k in (1, 3, 2):
        sends.append(
            push(wt.at[p, :, 0:384], in_part(r), w_s.at[k], w_r.at[r], dp, at_z(k))
        )
    for k in (1, 3, 2):
        sends.append(
            push(wt.at[p, :, 0:384], in_part(r), w_s.at[3 + k], w_r.at[r], dp, at_y(k))
        )

    mine = r // 2 == p

    @pl.when(mine)
    def _():
        for j in range(TEAM):
            t = 2 * j + r % 2

            @pl.when(t != r)
            def _():
                push(wt.at[j, :, 384:512], out_part(t), sc_s.at[j], sc_r, dp, t)

    keep_hid = pltpu.make_async_copy(hid, hid8.at[p], loc.at[1])
    keep_hid.start()
    keep_cot = pltpu.make_async_copy(cot, cot8.at[p], loc.at[2])
    keep_cot.start()
    for k, (dx, dc) in enumerate(((1, 0), (3, 0), (2, 0), (0, 1))):
        sends.append(
            push(hid, hid8.at[p], hid_s.at[k], hid_r.at[p], base + team(dx, dc), r)
        )
    for k in range(1, TEAM):
        sends.append(
            push(tab, tab8.at[p], tab_s.at[k], tab_r.at[p], base + lax.rem(p + k, TEAM), r)
        )

    for n, k in enumerate((1, 3, 2)):
        s = at_z(k)
        await_recv(in_part(s), w_r.at[s], dp, s)
        for m in (1, 3, 2):
            sends.append(
                push(in_part(s), in_part(s), w_s.at[7 + n * 3 + m], w_r.at[s], dp, at_y(m))
            )

    piece = out_part(r)

    @pl.when(mine)
    def _():
        copy = pltpu.make_async_copy(wt.at[p, :, 384:512], piece, loc.at[3])
        copy.start()
        copy.wait()

    @pl.when(jnp.logical_not(mine))
    def _():
        await_recv(piece, sc_r, dp, r)

    for k in (1, 3, 2):
        sends.append(push(piece, piece, o_s.at[k], o_r.at[r], dp, at_z(k)))
    for k in (1, 3, 2):
        sends.append(push(piece, piece, o_s.at[3 + k], o_r.at[r], dp, at_y(k)))

    for n, dx in enumerate((1, 3, 2)):
        i = team(dx, 0)
        await_recv(hid8.at[i], hid_r.at[i], base + i, r)
        sends.append(
            push(hid8.at[i], hid8.at[i], hid_s.at[4 + n], hid_r.at[i], base + team(0, 1), r)
        )
    for k, (dx, dc) in enumerate(((1, 0), (3, 0), (2, 0), (0, 1))):
        sends.append(
            push(cot, cot8.at[p], cot_s.at[k], cot_r.at[p], base + team(dx, dc), r)
        )
    for n, k in enumerate((1, 3, 2)):
        s = at_z(k)
        await_recv(out_part(s), o_r.at[s], dp, s)
        for m in (1, 3, 2):
            sends.append(
                push(out_part(s), out_part(s), o_s.at[7 + n * 3 + m], o_r.at[s], dp, at_y(m))
            )

    for m in (1, 3, 2):
        for k in range(4):
            s = lax.rem(zh + k, 4) * YS + lax.rem(y + m, YS)
            await_recv(in_part(s), w_r.at[s], dp, s)
    own.wait()
    keep_hid.wait()

    def deliver(i, e, half):
        t = 2 * i + e

        @pl.when(t != r)
        def _():
            push(
                stage.at[t, half], land.at[r, half], a_s.at[t, half], a_r.at[r, half], dp, t
            )

        @pl.when(t == r)
        def _():
            land[r, half] = stage[t, half]

    order = ((0, 0), (0, 1), (1, 0), (3, 0), (1, 1), (3, 1), (2, 0), (2, 1))
    for dx, dc in order:
        i = team(dx, dc)
        if dc == 1:
            await_recv(hid8.at[i], hid_r.at[i], base + i, r)
        qkv = dot(hid8[i], wg[:, 0:384]).astype(BF)
        q, k, v = qkv[:, 0:128], qkv[:, 128:256], qkv[:, 256:384]
        vals[i] = v
        stage[2 * i, 0] = merge(q, k)
        stage[2 * i + 1, 0] = merge_high(q, k)
        deliver(i, 0, 0)
        deliver(i, 1, 0)

    keep_cot.wait()
    for n, dx in enumerate((1, 3, 2)):
        i = team(dx, 0)
        await_recv(cot8.at[i], cot_r.at[i], base + i, r)
        sends.append(
            push(cot8.at[i], cot8.at[i], cot_s.at[4 + n], cot_r.at[i], base + team(0, 1), r)
        )
    for m in (1, 3, 2):
        for k in range(4):
            s = lax.rem(zh + k, 4) * YS + lax.rem(y + m, YS)
            await_recv(out_part(s), o_r.at[s], dp, s)
    for j in range(TEAM):
        wo[128 * j : 128 * j + 128, :] = wg[128 * j : 128 * j + 128, 384:512].T
    for dx, dc in order:
        i = team(dx, dc)
        if dc == 1:
            await_recv(cot8.at[i], cot_r.at[i], base + i, r)
        g = dot(cot8[i], wo[...]).astype(BF)
        v = vals[i]
        stage[2 * i, 1] = merge(v, g)
        stage[2 * i + 1, 1] = merge_high(v, g)
        deliver(i, 0, 1)
        deliver(i, 1, 1)

    for copy in sends:
        copy.wait_send()
    wg[:, 384:512] = wo[...]
    outs = [
        pltpu.make_async_copy(hid8, hid8_out, loc.at[0]),
        pltpu.make_async_copy(cot8, cot8_out, loc.at[1]),
        pltpu.make_async_copy(wg, wg_out, loc.at[2]),
    ]
    for copy in outs:
        copy.start()
    for k in range(1, TEAM):
        i = lax.rem(p + k, TEAM)
        await_recv(tab8.at[i], tab_r.at[i], base + i, r)
    tab8[p] = tab[...]
    tab_out[...] = tab8[r // 2]

    @pl.when(mine)
    def _():
        for j in range(TEAM):
            t = 2 * j + r % 2

            @pl.when(t != r)
            def _():
                pltpu.make_async_remote_copy(
                    src_ref=wt.at[j, :, 384:512],
                    dst_ref=out_part(t),
                    send_sem=sc_s.at[j],
                    recv_sem=sc_r,
                    device_id=(dp, t),
                    device_id_type=pl.DeviceIdType.MESH,
                ).wait_send()

    for k in range(1, SEQ):
        t = lax.rem(r + k, SEQ)
        for half in (0, 1):
            await_recv(land.at[t, half], a_r.at[t, half], dp, t)
            pltpu.make_async_remote_copy(
                src_ref=stage.at[t, half],
                dst_ref=land.at[r, half],
                send_sem=a_s.at[t, half],
                recv_sem=a_r.at[r, half],
                device_id=(dp, t),
                device_id_type=pl.DeviceIdType.MESH,
            ).wait_send()
    last = pltpu.make_async_copy(land, qg_out, loc.at[3])
    last.start()
    for copy in outs:
        copy.wait()
    last.wait()


def gather(hid, cot, wt, tab):
    any_ = pl.BlockSpec(memory_space=pl.ANY)
    vmem = pl.BlockSpec(memory_space=pltpu.VMEM)
    dma = pltpu.SemaphoreType.DMA
    shapes = [
        ((SEQ, 2, 128, 128), BF),
        ((TEAM, ROWS, WIDTH), BF),
        ((TEAM, ROWS, WIDTH), BF),
        ((WIDTH, 512), BF),
        ((8, 128), jnp.int32),
    ]
    return pl.pallas_call(
        gather_kernel,
        out_shape=[jax.ShapeDtypeStruct(s, d) for s, d in shapes],
        in_specs=[vmem] * 4,
        out_specs=[any_] * 4 + [vmem],
        scratch_shapes=[
            pltpu.VMEM((TEAM, ROWS, WIDTH), BF),
            pltpu.VMEM((TEAM, ROWS, WIDTH), BF),
            pltpu.VMEM((WIDTH, 512), BF),
            pltpu.VMEM((WIDTH, 128), BF),
            pltpu.VMEM((TEAM, 8, 128), jnp.int32),
            pltpu.VMEM((TEAM, 128, 128), BF),
            pltpu.VMEM((SEQ, 2, 128, 128), BF),
            pltpu.VMEM((SEQ, 2, 128, 128), BF),
            dma((8,)), dma((8,)), dma((8,)), dma((8,)), dma((8,)), dma((8,)),
            dma((17,)), dma((16,)), dma((17,)), dma((16,)), dma((8,)), dma(()),
            dma((16, 2)), dma((16, 2)), dma((4,)),
        ],
        compiler_params=pltpu.CompilerParams(
            collective_id=1, has_side_effects=True, vmem_limit_bytes=VMEM_BYTES
        ),
    )(hid, cot, wt, tab)


def attend_kernel(tab, a, out, acc, slot_of):
    for s in range(SEQ):
        slot_of[tab[0, s]] = s
    acc[...] = jnp.zeros_like(acc)
    lo = low_lanes((128, 128))
    zero = jnp.zeros((128, 128), BF)

    def step(s, carry):
        qk, vg = a[s, 0], a[s, 1]
        qz = jnp.where(lo, zero, pltpu.roll(qk, 64, 1)) * jnp.asarray(0.125, BF)
        gz = jnp.where(lo, pltpu.roll(vg, 64, 1), zero)
        rhs = jnp.concatenate([jnp.where(lo, qk, zero), jnp.where(lo, zero, vg)], axis=0)
        count = tab[0, 80 + s]
        slots = [slot_of[tab[0, 16 + 4 * s + j]] for j in range(4)]
        keys = [a[b, 0] for b in slots]
        vals = [a[b, 1] for b in slots]
        scores = [
            jnp.where(j < count, dot(k, qz, NT), -1e30) for j, k in enumerate(keys)
        ]
        grad_p = [dot(v, gz, NT) for v in vals]
        top = jnp.max(
            jnp.maximum(jnp.maximum(scores[0], scores[1]), jnp.maximum(scores[2], scores[3])),
            axis=0,
            keepdims=True,
        )
        expo = [jnp.exp(v - top) for v in scores]
        total = jnp.sum((expo[0] + expo[1]) + (expo[2] + expo[3]), axis=0, keepdims=True)
        inv = 1.0 / total
        probs = [e * inv for e in expo]
        prod = [p * g for p, g in zip(probs, grad_p)]
        delta = jnp.sum((prod[0] + prod[1]) + (prod[2] + prod[3]), axis=0, keepdims=True)
        low = [p.astype(BF) for p in probs]
        grad_s = [
            (p * (g - delta) * 0.125).astype(BF) for p, g in zip(probs, grad_p)
        ]
        attn = dot(jnp.concatenate(low, axis=0), jnp.concatenate(vals, axis=0), TN)
        grad_q = dot(jnp.concatenate(grad_s, axis=0), jnp.concatenate(keys, axis=0), TN)
        out[s, 0] = jnp.where(lo, attn, grad_q).astype(BF)
        for j in range(4):
            acc[slots[j]] += dot(jnp.concatenate([grad_s[j], low[j]], axis=1), rhs)
        return carry

    lax.fori_loop(0, SEQ, step, 0)
    for s in range(SEQ):
        out[s, 1] = acc[s].astype(BF)


def attend(tab, a):
    vmem = pl.BlockSpec(memory_space=pltpu.VMEM)
    return pl.pallas_call(
        attend_kernel,
        out_shape=jax.ShapeDtypeStruct((SEQ, 2, 128, 128), BF),
        in_specs=[pl.BlockSpec(memory_space=pltpu.SMEM), vmem],
        out_specs=vmem,
        scratch_shapes=[pltpu.VMEM((SEQ, 128, 128), F32), pltpu.SMEM((SEQ,), jnp.int32)],
        compiler_params=pltpu.CompilerParams(vmem_limit_bytes=VMEM_BYTES),
    )(tab, a)


def finish_kernel(
    ao, hid8_in, cot8_in, wg_in,
    layer_out, features_grad, proj_grad,
    hid8, cot8, wg, land, mix, part, sib, far, terms, from_y, to_z, from_z, from_zl, full, wob,
    a_s, a_r, sib_s, sib_r, far_s, far_r, y_s, y_r, z_s, z_r, zl_s, zl_r, g_s, g_r, o_s, o_r, loc,
):
    zl, p, r = place()
    x, c = p // 2, p % 2
    zh, y = r // YS, r % YS
    base = zl * TEAM
    dp = base + p
    other = lax.rem(dp + TEAM, 2 * TEAM)

    def team(dx, dc):
        return lax.rem(x + dx, XS) * 2 + lax.rem(c + dc, 2)

    loads = [
        pltpu.make_async_copy(wg_in, wg, loc.at[0]),
        pltpu.make_async_copy(hid8_in, hid8, loc.at[1]),
        pltpu.make_async_copy(cot8_in, cot8, loc.at[2]),
    ]
    for copy in loads:
        copy.start()
    greet(
        [(base + lax.rem(p + k, TEAM), r) for k in range(1, TEAM)]
        + [(dp, lax.rem(r + k, SEQ)) for k in range(1, SEQ)]
        + [(other, r)]
    )
    sends = []
    for k in range(1, SEQ):
        t = lax.rem(r + k, SEQ)
        sends.append(push(ao.at[t], land.at[r], a_s.at[k], a_r.at[r], dp, t))
    land[r] = ao[r]
    for copy in loads:
        copy.wait()

    def arrive(t):
        @pl.when(t != r)
        def _():
            await_recv(land.at[t], a_r.at[t], dp, t)

    def work(i):
        arrive(2 * i)
        arrive(2 * i + 1)
        a0, a1 = land[2 * i, 0], land[2 * i + 1, 0]
        b0, b1 = land[2 * i, 1], land[2 * i + 1, 1]
        attn = merge(a0, a1)
        grads = jnp.concatenate([merge_high(a0, a1), merge(b0, b1), merge_high(b0, b1)], axis=1)
        rows = pl.ds(pl.multiple_of(i * ROWS, ROWS), ROWS)
        mix[rows, 0:128] = attn
        mix[rows, 128:512] = grads
        return dot(attn, wg[:, 384:512], NT), dot(grads, wg[:, 0:384], NT)

    for n, dx in enumerate((1, 3, 2, 0)):
        lo, fg = work(team(dx, 1))
        part[n, 0] = lo.astype(BF)
        part[n, 1] = fg.astype(BF)
        sends.append(
            push(part.at[n], sib.at[n], sib_s.at[n], sib_r.at[n], base + team(0, 1), r)
        )
    for n, dx in enumerate((1, 3, 2, 0)):
        i = team(dx, 0)
        lo, fg = work(i)
        await_recv(sib.at[n], sib_r.at[n], base + team(0, 1), r)
        lo += sib[n, 0].astype(F32)
        fg += sib[n, 1].astype(F32)
        if dx:
            part[4 + n, 0] = lo.astype(BF)
            part[4 + n, 1] = fg.astype(BF)
            sends.append(
                push(part.at[4 + n], far.at[n], far_s.at[n], far_r.at[n], base + i, r)
            )

    out_term = dot(mix[:, 0:128], cot8[...].reshape(TEAM * ROWS, WIDTH), TN)
    for j in range(TEAM):
        block = out_term[:, 128 * j : 128 * j + 128].astype(BF)
        terms[2 * j, :, 384:512] = block[0:64]
        terms[2 * j + 1, :, 384:512] = block[64:128]
    for h in range(4):
        hidden = hid8[:, :, 256 * h : 256 * h + 256].reshape(TEAM * ROWS, 256)
        in_term = dot(hidden, mix[:, 128:512], TN)
        for m in range(YS):
            terms[4 * h + m, :, 0:384] = in_term[64 * m : 64 * m + 64].astype(BF)
        for k in (1, 3, 2):
            t = lax.rem(y + k, YS)
            sends.append(
                push(
                    terms.at[4 * h + t], from_y.at[y, h], y_s.at[k, h], y_r.at[y, h],
                    dp, zh * YS + t,
                )
            )

    for n in range(3):
        await_recv(far.at[n], far_r.at[n], dp, r)
        lo += far[n, 0].astype(F32)
        fg += far[n, 1].astype(F32)
    layer_out[...] = (hid8[p].astype(F32) + lo).astype(BF)
    features_grad[...] = (cot8[p].astype(F32) + fg).astype(BF)

    for k in (1, 2, 3, 0):
        h = lax.rem(zh + k, 4)
        total = terms[4 * h + y].astype(F32)
        for m in (1, 3, 2):
            t = lax.rem(y + m, YS)
            await_recv(from_y.at[t, h], y_r.at[t, h], dp, r)
            total += from_y[t, h].astype(F32)
        if k:
            to_z[h] = total.astype(BF)
            sends.append(
                push(to_z.at[h], from_z.at[zh], z_s.at[h], z_r.at[zh], dp, h * YS + y)
            )
    for k in (1, 3, 2):
        h = lax.rem(zh + k, 4)
        await_recv(from_z.at[h], z_r.at[h], dp, r)
        total += from_z[h].astype(F32)
    to_z[zh] = total.astype(BF)
    sends.append(push(to_z.at[zh], from_zl, zl_s, zl_r, other, r))
    await_recv(from_zl, zl_r, other, r)
    full[p] = (to_z[zh].astype(F32) + from_zl[...].astype(F32)).astype(BF)

    for k in range(1, TEAM):
        i = lax.rem(p + k, TEAM)
        sends.append(push(full.at[p], full.at[p], g_s.at[k], g_r.at[p], base + i, r))
    for k in range(TEAM):
        i = lax.rem(p + k, TEAM)
        if k:
            await_recv(full.at[i], g_r.at[i], base + i, r)
        t = 2 * i + r % 2

        @pl.when(t != r)
        def _():
            push(full.at[i, :, 384:512], wob.at[r // 2], o_s.at[i], o_r.at[r // 2], dp, t)

        @pl.when(t == r)
        def _():
            wob[r // 2] = full[i, :, 384:512]

    for i in range(TEAM):
        for n in range(3):
            proj_grad[n, :, 128 * i : 128 * i + 128] = full[
                i, :, 128 * n : 128 * n + 128
            ].astype(F32)
    for j in range(TEAM):
        t = 2 * j + r % 2

        @pl.when(t != r)
        def _():
            await_recv(wob.at[j], o_r.at[j], dp, t)
            pltpu.make_async_remote_copy(
                src_ref=full.at[j, :, 384:512],
                dst_ref=wob.at[r // 2],
                send_sem=o_s.at[j],
                recv_sem=o_r.at[r // 2],
                device_id=(dp, t),
                device_id_type=pl.DeviceIdType.MESH,
            ).wait_send()

        proj_grad[3, :, 128 * j : 128 * j + 128] = wob[j].astype(F32)
    for copy in sends:
        copy.wait_send()


def finish(ao, hid8, cot8, wg):
    any_ = pl.BlockSpec(memory_space=pl.ANY)
    vmem = pl.BlockSpec(memory_space=pltpu.VMEM)
    dma = pltpu.SemaphoreType.DMA
    return pl.pallas_call(
        finish_kernel,
        out_shape=[
            jax.ShapeDtypeStruct((ROWS, WIDTH), BF),
            jax.ShapeDtypeStruct((ROWS, WIDTH), BF),
            jax.ShapeDtypeStruct((4, SHARD, WIDTH), F32),
        ],
        in_specs=[vmem, any_, any_, any_],
        out_specs=[vmem] * 3,
        scratch_shapes=[
            pltpu.VMEM((TEAM, ROWS, WIDTH), BF),
            pltpu.VMEM((TEAM, ROWS, WIDTH), BF),
            pltpu.VMEM((WIDTH, 512), BF),
            pltpu.VMEM((SEQ, 2, 128, 128), BF),
            pltpu.VMEM((TEAM * ROWS, 512), BF),
            pltpu.VMEM((7, 2, ROWS, WIDTH), BF),
            pltpu.VMEM((4, 2, ROWS, WIDTH), BF),
            pltpu.VMEM((3, 2, ROWS, WIDTH), BF),
            pltpu.VMEM((SEQ, SHARD, 512), BF),
            pltpu.VMEM((4, 4, SHARD, 512), BF),
            pltpu.VMEM((4, SHARD, 512), BF),
            pltpu.VMEM((4, SHARD, 512), BF),
            pltpu.VMEM((SHARD, 512), BF),
            pltpu.VMEM((TEAM, SHARD, 512), BF),
            pltpu.VMEM((TEAM, SHARD, 128), BF),
            dma((16,)), dma((16,)), dma((4,)), dma((4,)), dma((3,)), dma((3,)),
            dma((4, 4)), dma((4, 4)), dma((4,)), dma((4,)), dma(()), dma(()),
            dma((8,)), dma((8,)), dma((8,)), dma((8,)), dma((3,)),
        ],
        compiler_params=pltpu.CompilerParams(
            collective_id=2, has_side_effects=True, vmem_limit_bytes=VMEM_BYTES
        ),
    )(ao, hid8, cot8, wg)


def per_device(
    features, labels, label_table, proj_weight, block_order, neighbours, counts, cotangent
):
    onehot = (labels[0][:, None] == lax.iota(jnp.int32, label_table.shape[0])[None, :]).astype(BF)
    hidden = (
        features[0].astype(F32) + jnp.dot(onehot, label_table, preferred_element_type=F32)
    ).astype(BF)
    wt = proj_weight.reshape(SHARD, 4, TEAM, 128).transpose(2, 0, 1, 3).reshape(TEAM, SHARD, 512)
    tab = jnp.concatenate(
        [
            block_order[0],
            neighbours[0].reshape(-1),
            counts[0],
            jnp.zeros((32,), jnp.int32),
        ]
    )
    tab = jnp.broadcast_to(tab[None, :], (8, 128))
    qg, hid8, cot8, wg, table = gather(hidden, cotangent[0], wt, tab)
    ao = attend(table, qg)
    layer_out, features_grad, proj_grad = finish(ao, hid8, cot8, wg)
    return (layer_out[None], features_grad[None], proj_grad.transpose(1, 0, 2))


def solution(mesh):
    placed = (
        P("dp", "seq", None),
        P("dp", "seq"),
        P(),
        P("seq", None, None),
        P("dp", None),
        P("dp", None, None),
        P("dp", None),
        P("dp", "seq", None),
    )
    return jax.shard_map(
        per_device,
        mesh=mesh,
        in_specs=placed,
        out_specs=(P("dp", "seq", None), P("dp", "seq", None), P("seq", None, None)),
        check_vma=False,
    )
```

time: 554 us -> 156 us (0.28)
  waiting for transfers between devices: 380 us -> 0 us
  Pallas kernels: 0 us -> 148 us
  matrix products: 55.4 us -> 1.34 us
  local copies, waits for them, and re-layouts: 53 us -> 4.37 us
  starting transfers between devices: 37.8 us -> 0 us
  between operations: 14 us -> 0.72 us
  other arithmetic: 12.6 us -> 0.75 us
    pallas_call x0 -> x3, Pallas kernels: none -> 148 us  [the longest x1 86.9 us: finish(): pl.pallas_call(finish_kernel, out_shape=[jax.ShapeDtypeStruct((ROWS, WIDT...]
    reduce_scatter x1 -> x0, waiting for transfers between devices: 119 us -> none  [per_device(): lax.psum_scatter(jnp.concatenate([lax.dot_general(hidden, grad_qkv, contr...]
    all_gather x1 -> x0, waiting for transfers between devices: 116 us -> none  [per_device(): weights = lax.all_gather(proj_weight, 'seq', axis=0, tiled=True)]
    psum x1 -> x0, waiting for transfers between devices: 115 us -> none  [per_device(): lax.psum(lax.psum_scatter(jnp.concatenate([lax.dot_general(hidden, grad_q...]
    dot_general x43 -> x1, matrix products: 55.4 us -> 1.34 us  [per_device(): jnp.dot(onehot, label_table, preferred_element_type=F32)]
    all_to_all x4 -> x0, starting transfers between devices: 37.6 us -> none  [the longest x1 12 us: per_device(): lax.all_to_all(qkv, 'seq', split_axis=2, concat_axis=0, tiled=True)]
    all_to_all x4 -> x0, waiting for transfers between devices: 28.7 us -> none  [the longest x1 18.8 us: per_device(): lax.all_to_all(stacked, 'seq', split_axis=0, concat_axis=2, tiled=True)]
    unnamed x28 -> x8, local copies, waits for them, and re-layouts: 20.2 us -> 3.89 us
  transfers between devices with their start and end apart: 7 -> 0, of which waited for: 5 -> 0; matrix products, arithmetic and copies ran while one was open for 16% -> 0% of each run, Pallas kernels for 0% -> 0%
where the time goes in v1:
time: 156 us; the launch traced here: 155 us
  Pallas kernels  148 us (95%)
  local copies, waits for them, and re-layouts  4.37 us (3%)
    pallas_call x1, Pallas kernels, finish(): pl.pallas_call(finish_kernel, out_shape=[jax.ShapeDtypeStruct((ROWS, WIDT...  86.9 us
    pallas_call x1, Pallas kernels, gather(): pl.pallas_call(gather_kernel, out_shape=[jax.ShapeDtypeStruct(s, d) for s...  48.4 us
    pallas_call x1, Pallas kernels, attend(): pl.pallas_call(attend_kernel, out_shape=jax.ShapeDtypeStruct((SEQ, 2, 128...  13 us
    unnamed x8, local copies, waits for them, and re-layouts  3.89 us

profile of v1, /device:TPU:1, one launch (start us, length us, event | category | flops | bytes accessed | tf_op | source)
XLA Modules:
  0.0 155.5 jit_solution(14035549116378243861)
XLA Ops:
  0.6 0.0 copy-start
  0.6 0.0 copy-start.1
  0.7 0.8 copy.15
  1.5 0.1 reshape_squeeze.3
  1.6 0.8 pad_add_fusion
  2.3 1.3 fusion.hid
  3.7 0.0 copy-done
  3.7 0.2 bitcast_bitcast_fusion
  3.9 0.2 reshape.17.wt
  4.1 0.0 copy-done.1
  4.1 48.4 %shard_map.103 = (bf16[16,2,128,128]{3,2,1,0:T(8,128)(2,1)S(1)}, bf16[8,128,1024]{2,1,0:T(8,128)(2,1)S(1)}, bf16[8,128,1024]{2,1,0:T(8,128)(2,1)}, bf16[1024,512]{1,0:T(8,128)(2,1)S(1)}, s32[8,128]{1,0:T(8,128)S(1)}) custom-call(bf16[128,1024]{1,0:T(8,128)(2,1)S(1)} %fusion.hid, bf16[128,1024]{1,0:T(8,128)(2,1)S(1)} %bitcast.21, ...), custom_call_target="tpu_custom_call" | custom-call | tf_op jit(solution)/shard_map/pallas_call | solution.py:304
  52.5 13.0 %shard_map.104.ao = bf16[16,2,128,128]{3,2,1,0:T(8,128)(2,1)S(1)} custom-call(s32[8,128]{1,0:T(8,128)S(1)} %get-tuple-element.11.tab, bf16[16,2,128,128]{3,2,1,0:T(8,128)(2,1)S(1)} %get-tuple-element.12.a), custom_call_target="tpu_custom_call" | custom-call | tf_op jit(solution)/shard_map/pallas_call | solution.py:377
  65.5 86.9 %shard_map.105 = (bf16[128,1024]{1,0:T(8,128)(2,1)S(1)}, bf16[128,1024]{1,0:T(8,128)(2,1)S(1)}, f32[4,64,1024]{2,1,0:T(8,128)S(1)}) custom-call(bf16[16,2,128,128]{3,2,1,0:T(8,128)(2,1)S(1)} %shard_map.104.ao, bf16[8,128,1024]{2,1,0:T(8,128)(2,1)S(1)} %get-tuple-element.13.hid8_in, bf16[8,128,1024]{2,1,0:T(8,128)(2,1)} %get-tuple-element.14.cot8_in, ...), custom_call_target="tpu_custom_call" | custom-call | tf_op jit(solution)/shard_map/pallas_call | solution.py:553
  152.4 1.6 %copy.16 = f32[64,4,1024]{2,1,0:T(4,128)} copy(f32[64,4,1024]{2,0,1:T(8,128)S(1)} %bitcast.18) | data formatting | bytes 2097152
  154.1 0.7 copy.21
  154.8 0.7 copy.22
  (2 shorter events, 0.0 us)
Async XLA Ops:
  0.6 3.1 %copy-start = (bf16[64,4,1024]{2,1,0:T(4,128)(2,1)S(1)}, bf16[64,4,1024]{2,1,0:T(4,128)(2,1)}, u32[]{:S(2)}) copy-start(bf16[64,4,1024]{2,1,0:T(4,128)(2,1)} %param.11) | copy-start | bytes 1572868
  0.6 3.5 %copy-start.1 = (bf16[1,128,1024]{2,1,0:T(8,128)(2,1)S(1)}, bf16[1,128,1024]{2,1,0:T(8,128)(2,1)}, u32[]{:S(2)}) copy-start(bf16[1,128,1024]{2,1,0:T(8,128)(2,1)} %param.15) | copy-start | bytes 786436

commit v2 on v0

v2 whole, which is shorter than its diff:
```python
import jax
import jax.numpy as jnp
from jax import lax
from jax.experimental import pallas as pl
from jax.experimental.pallas import tpu as pltpu
from jax.sharding import PartitionSpec as P

XS, YS, TEAM, SEQ, ROWS, WIDTH = 4, 4, 8, 16, 128, 1024
SHARD = WIDTH // SEQ
HALF = 4 * ROWS
BF, F32 = jnp.bfloat16, jnp.float32
NN = (((1,), (0,)), ((), ()))
NT = (((1,), (1,)), ((), ()))
TN = (((0,), (0,)), ((), ()))
VMEM_BYTES = 40 << 20
MESH = pl.DeviceIdType.MESH
NEAR = (1, 3, 2)


def dot(a, b, dims=NN):
    return lax.dot_general(a, b, dims, preferred_element_type=F32)


def remote(src, dst, send, recv, where):
    return pltpu.make_async_remote_copy(
        src_ref=src, dst_ref=dst, send_sem=send, recv_sem=recv, device_id=where, device_id_type=MESH
    )


def push(src, dst, send, recv, where):
    copy = remote(src, dst, send, recv, where)
    copy.start()
    return copy


def arrival(dst, recv, where):
    remote(dst, dst, recv, recv, where).wait_recv()


def low_lanes(shape):
    return lax.broadcasted_iota(jnp.int32, shape, 1) < 64


def merge(a, b):
    return jnp.where(low_lanes(a.shape), a, pltpu.roll(b, 64, 1))


def merge_high(a, b):
    return jnp.where(low_lanes(a.shape), pltpu.roll(a, 64, 1), b)


def kernel(
    hid, cot, wt, tab,
    layer_out, features_grad, proj_grad,
    hid8, cot8, hid_t, wg, wo, w_t, tab8, tabs, stage, land_qk, land_vg, probs, tiles, back, home, mix,
    part, sib, far, terms, from_y, to_z, from_z, from_zl, full, wob,
    hid_s, hid_r, cot_s, cot_r, tab_s, tab_r, w_s, w_r, v_s, v_r, o_s, o_r, sc_s, sc_r, a_s, a_r, b_s, b_r,
    sib_s, sib_r, far_s, far_r, y_s, y_r, z_s, z_r, zl_s, zl_r, g_s, g_r, q_s, q_r, loc,
):
    dp, r = lax.axis_index("dp"), lax.axis_index("seq")
    zl, p = dp // TEAM, dp % TEAM
    x, c = p // 2, p % 2
    zh, y = r // YS, r % YS
    base = zl * TEAM
    me = c * XS + x
    sibling = (base + x * 2 + 1 - c, r)
    partner = (lax.rem(dp + TEAM, 2 * TEAM), r)

    def turn(k):
        return lax.rem(x + k, XS)

    def slot(k):
        return c * XS + turn(k)

    def at_x(k):
        return (base + turn(k) * 2 + c, r)

    def at_z(k):
        return lax.rem(zh + k, 4) * YS + y

    def at_y(k):
        return zh * YS + lax.rem(y + k, YS)

    def team_peer(k):
        return base + lax.rem(p + k, TEAM)

    def slot_of(q):
        return lax.rem(q, 2) * XS + q // 2

    barrier = pltpu.get_barrier_semaphore()
    greeted = [(team_peer(k), r) for k in range(1, TEAM)]
    greeted += [(dp, lax.rem(r + k, SEQ)) for k in range(1, SEQ)] + [partner]
    for where in greeted:
        pl.semaphore_signal(barrier, inc=1, device_id=where, device_id_type=MESH)
    pl.semaphore_wait(barrier, len(greeted))
    sends = []
    land = (land_qk, land_vg)

    def rows_of(s):
        return pl.ds(pl.multiple_of(s * SHARD, SHARD), SHARD)

    def qk_part(s):
        return wg.at[rows_of(s), 0:256]

    def v_part(s):
        return wg.at[rows_of(s), 256:384]

    def out_part(s):
        return wg.at[rows_of(s), 384:512]

    own_w = pltpu.make_async_copy(wt.at[p, :, 0:384], wg.at[rows_of(r), 0:384], loc.at[0])
    own_w.start()
    mine_qk, mine_v = wt.at[p, :, 0:256], wt.at[p, :, 256:384]
    for k in NEAR:
        sends.append(push(mine_qk, qk_part(r), w_s.at[k], w_r.at[r], (dp, at_z(k))))
        sends.append(push(mine_v, v_part(r), v_s.at[k], v_r.at[r], (dp, at_y(k))))
    for k in NEAR:
        sends.append(push(mine_qk, qk_part(r), w_s.at[3 + k], w_r.at[r], (dp, at_y(k))))
        sends.append(push(mine_v, v_part(r), v_s.at[3 + k], v_r.at[r], (dp, at_z(k))))

    spread = r // 2 == p

    @pl.when(spread)
    def _():
        for j in range(TEAM):
            t = 2 * j + r % 2

            @pl.when(t != r)
            def _():
                push(wt.at[j, :, 384:512], out_part(t), sc_s.at[j], sc_r, (dp, t))

    keep_hid = pltpu.make_async_copy(hid, hid8.at[me], loc.at[1])
    keep_hid.start()
    keep_cot = pltpu.make_async_copy(cot, cot8.at[me], loc.at[2])
    keep_cot.start()
    for k in NEAR:
        sends.append(push(hid, hid8.at[me], hid_s.at[k], hid_r.at[me], at_x(k)))
    sends.append(push(hid, hid8.at[me], hid_s.at[0], hid_r.at[me], sibling))
    for k in range(1, TEAM):
        sends.append(push(tab, tab8.at[me], tab_s.at[k], tab_r.at[me], (team_peer(k), r)))

    for n, k in enumerate(NEAR):
        s = at_z(k)
        arrival(qk_part(s), w_r.at[s], (dp, s))
        for m in NEAR:
            sends.append(
                push(qk_part(s), qk_part(s), w_s.at[7 + n * 3 + m], w_r.at[s], (dp, at_y(m)))
            )
        s = at_y(k)
        arrival(v_part(s), v_r.at[s], (dp, s))
        for m in NEAR:
            sends.append(
                push(v_part(s), v_part(s), v_s.at[7 + n * 3 + m], v_r.at[s], (dp, at_z(m)))
            )

    piece = out_part(r)

    @pl.when(spread)
    def _():
        copy = pltpu.make_async_copy(wt.at[p, :, 384:512], piece, loc.at[3])
        copy.start()
        copy.wait()

    @pl.when(jnp.logical_not(spread))
    def _():
        arrival(piece, sc_r, (dp, r))

    for k in NEAR:
        sends.append(push(piece, piece, o_s.at[k], o_r.at[r], (dp, at_z(k))))
    for k in NEAR:
        sends.append(push(piece, piece, o_s.at[3 + k], o_r.at[r], (dp, at_y(k))))

    for n, k in enumerate(NEAR):
        q = slot(k)
        arrival(hid8.at[q], hid_r.at[q], at_x(k))
        sends.append(push(hid8.at[q], hid8.at[q], hid_s.at[4 + n], hid_r.at[q], sibling))
    for k in NEAR:
        sends.append(push(cot, cot8.at[me], cot_s.at[k], cot_r.at[me], at_x(k)))
    sends.append(push(cot, cot8.at[me], cot_s.at[0], cot_r.at[me], sibling))
    for n, k in enumerate(NEAR):
        s = at_z(k)
        arrival(out_part(s), o_r.at[s], (dp, s))
        for m in NEAR:
            sends.append(
                push(out_part(s), out_part(s), o_s.at[7 + n * 3 + m], o_r.at[s], (dp, at_y(m)))
            )

    def from_all_y(piece_of, sems):
        for m in NEAR:
            for k in range(4):
                s = lax.rem(zh + k, 4) * YS + lax.rem(y + m, YS)
                arrival(piece_of(s), sems.at[s], (dp, s))

    from_all_y(qk_part, w_r)
    own_w.wait()
    keep_hid.wait()

    def deliver(t, half):
        @pl.when(t != r)
        def _():
            push(
                stage.at[t, half], land[half].at[r], a_s.at[t, half], a_r.at[r, half], (dp, t)
            )

        @pl.when(t == r)
        def _():
            land[half][r] = stage[t, half]

    def group_rows(array, core):
        block = array[pl.ds(pl.multiple_of(core * XS, XS), XS)]
        return block.reshape(HALF, array.shape[2])

    for core in (c, 1 - c):
        if core is not c:
            for k in range(XS):
                q = (1 - c) * XS + turn(k)
                arrival(hid8.at[q], hid_r.at[q], sibling)
        queries_keys = dot(group_rows(hid8, core), wg[:, 0:256]).astype(BF)
        for n in range(XS):
            rows = queries_keys[n * ROWS : n * ROWS + ROWS]
            q, k = rows[:, 0:128], rows[:, 128:256]
            i = core * XS + n
            stage[2 * i, 0] = merge(q, k)
            stage[2 * i + 1, 0] = merge_high(q, k)
            deliver(2 * i, 0)
            deliver(2 * i + 1, 0)

    keep_cot.wait()
    for n, k in enumerate(NEAR):
        q = slot(k)
        arrival(cot8.at[q], cot_r.at[q], at_x(k))
        sends.append(push(cot8.at[q], cot8.at[q], cot_s.at[4 + n], cot_r.at[q], sibling))
    for m in NEAR:
        for k in range(1, 4):
            s = lax.rem(zh + k, 4) * YS + lax.rem(y + m, YS)
            arrival(v_part(s), v_r.at[s], (dp, s))
    for k in NEAR:
        s = at_z(k)
        arrival(v_part(s), v_r.at[s], (dp, s))
    from_all_y(out_part, o_r)
    for j in range(TEAM):
        block = wg[128 * j : 128 * j + 128, 384:512]
        wo[128 * j : 128 * j + 128, :] = block.T
        w_t[384:512, 128 * j : 128 * j + 128] = block
    for core in (c, 1 - c):
        if core is not c:
            for k in range(XS):
                q = (1 - c) * XS + turn(k)
                arrival(cot8.at[q], cot_r.at[q], sibling)
        values = dot(group_rows(hid8, core), wg[:, 256:384]).astype(BF)
        grad = dot(group_rows(cot8, core), wo[...]).astype(BF)
        for n in range(XS):
            g = grad[n * ROWS : n * ROWS + ROWS]
            v = values[n * ROWS : n * ROWS + ROWS]
            i = core * XS + n
            stage[2 * i, 1] = merge(v, g)
            stage[2 * i + 1, 1] = merge_high(v, g)
            deliver(2 * i, 1)
            deliver(2 * i + 1, 1)

    for n in range(3):
        w_t[128 * n : 128 * n + 128, :] = wg[:, 128 * n : 128 * n + 128].T
    for q in range(TEAM):
        hid_t[:, 128 * q : 128 * q + 128] = hid8[q].T

    for k in range(1, TEAM):
        i = lax.rem(p + k, TEAM)
        q = slot_of(i)
        arrival(tab8.at[q], tab_r.at[q], (base + i, r))
    tab8[me] = tab[...]
    to_scalars = pltpu.make_async_copy(tab8.at[r // 2], tabs, loc.at[3])
    to_scalars.start()
    to_scalars.wait()

    def all_landed(half):
        def one(k, carry):
            t = lax.rem(r + k, SEQ)
            arrival(land[half].at[t], a_r.at[t, half], (dp, t))
            return carry

        lax.fori_loop(1, SEQ, one, 0)

    lo = low_lanes((128, 128))
    zero = jnp.zeros((128, 128), BF)
    all_landed(0)

    def probabilities(s):
        qz = jnp.where(lo, zero, pltpu.roll(land_qk[s], 64, 1)) * jnp.asarray(0.125, BF)
        count = tabs[2, 64 + s]
        scores = [
            jnp.where(j < count, dot(land_qk[tabs[2, 4 * s + j]], qz, NT), -1e30) for j in range(4)
        ]
        top = jnp.max(
            jnp.maximum(jnp.maximum(scores[0], scores[1]), jnp.maximum(scores[2], scores[3])),
            axis=0,
            keepdims=True,
        )
        expo = [jnp.exp(v - top) for v in scores]
        total = jnp.sum((expo[0] + expo[1]) + (expo[2] + expo[3]), axis=0, keepdims=True)
        inv = 1.0 / total
        for j in range(4):
            probs[s, j] = expo[j] * inv

    def forward(g, carry):
        for n in range(4):
            probabilities(4 * g + n)
        return carry

    lax.fori_loop(0, 4, forward, 0)
    all_landed(1)

    def give_back(s, half):
        @pl.when(s != r)
        def _():
            push(back.at[s, half], home.at[r, half], b_s.at[s, half], b_r.at[r, half], (dp, s))

        @pl.when(s == r)
        def _():
            home[r, half] = back[s, half]

    def gradients(s):
        qk, vg = land_qk[s], land_vg[s]
        gz = jnp.where(lo, pltpu.roll(vg, 64, 1), zero)
        rhs = jnp.concatenate([jnp.where(lo, qk, zero), jnp.where(lo, zero, vg)], axis=0)
        slots = [tabs[2, 4 * s + j] for j in range(4)]
        keys = [land_qk[b] for b in slots]
        values = [land_vg[b] for b in slots]
        grad_p = [dot(v, gz, NT) for v in values]
        prob = [probs[s, j] for j in range(4)]
        prod = [a * g for a, g in zip(prob, grad_p)]
        delta = jnp.sum((prod[0] + prod[1]) + (prod[2] + prod[3]), axis=0, keepdims=True)
        low = [a.astype(BF) for a in prob]
        grad_s = [(a * (g - delta) * 0.125).astype(BF) for a, g in zip(prob, grad_p)]
        attn = dot(jnp.concatenate(values, axis=0), jnp.concatenate(low, axis=0), TN)
        grad_q = dot(jnp.concatenate(keys, axis=0), jnp.concatenate(grad_s, axis=0), TN)
        back[s, 0] = jnp.concatenate([attn[0:64], grad_q[64:128]], axis=0).T.astype(BF)
        for j in range(4):
            tiles[4 * s + j] = dot(jnp.concatenate([grad_s[j], low[j]], axis=1), rhs)

    def backward(g, carry):
        blocks = [lax.rem(r + 1 + 4 * g + n, SEQ) for n in range(4)]
        for s in blocks:
            gradients(s)
        for s in blocks:
            give_back(s, 0)
        return carry

    lax.fori_loop(0, 4, backward, 0)
    tiles[64] = jnp.zeros((128, 128), F32)

    def collect(n, carry):
        b = lax.rem(r + 1 + n, SEQ)
        total = tiles[tabs[b // 8, (b % 8) * 16]]
        for s in range(1, SEQ):
            total += tiles[tabs[b // 8, (b % 8) * 16 + s]]
        back[b, 1] = total.astype(BF)
        give_back(b, 1)
        return carry

    lax.fori_loop(0, SEQ, collect, 0)

    def came_home(t, half):
        @pl.when(t != r)
        def _():
            arrival(home.at[t, half], b_r.at[t, half], (dp, t))

    def half_rows(core):
        return pl.ds(pl.multiple_of(core * HALF, HALF), HALF)

    def take(core, half):
        for n in range(XS):
            i = core * XS + n
            came_home(2 * i, half)
            came_home(2 * i + 1, half)
            a, b = home[2 * i, half], home[2 * i + 1, half]
            rows = pl.ds(pl.multiple_of(i * ROWS, ROWS), ROWS)
            mix[rows, 256 * half : 256 * half + 128] = merge(a, b)
            mix[rows, 256 * half + 128 : 256 * half + 256] = merge_high(a, b)

    def product(core, n):
        if n == 0:
            return dot(mix[half_rows(core), 0:128], w_t[384:512, :])
        return dot(mix[half_rows(core), 128:512], w_t[0:384, :])

    def share(n):
        result = product(1 - c, n).astype(BF)
        for i in range(XS):
            part[n, i] = result[i * ROWS : i * ROWS + ROWS]
        sends.append(push(part.at[n, 0:XS], sib.at[n], sib_s.at[n], sib_r.at[n], sibling))

    def pass_on(n):
        result = product(c, n)
        arrival(sib.at[n], sib_r.at[n], sibling)
        for i in range(XS):
            total = result[i * ROWS : i * ROWS + ROWS] + sib[n, i].astype(F32)
            part[n, XS + i] = total.astype(BF)
        for k in NEAR:
            sends.append(
                push(
                    part.at[n, XS + turn(k)], far.at[n, x], far_s.at[n, k], far_r.at[n, x], at_x(k)
                )
            )

    def result_of(n, first):
        total = first.astype(F32) + part[n, XS + x].astype(F32)
        for k in NEAR:
            arrival(far.at[n, turn(k)], far_r.at[n, turn(k)], at_x(k))
            total += far[n, turn(k)].astype(F32)
        return total.astype(BF)

    def terms_out(n):
        if n == 0:
            cots = cot8[...].reshape(TEAM * ROWS, WIDTH)
            out_term = dot(mix[:, 0:128], cots, TN).astype(BF)
            for j in range(TEAM):
                block = out_term[:, 128 * j : 128 * j + 128]
                terms[0, 2 * j, :, 128:256] = block[0:64]
                terms[0, 2 * j + 1, :, 128:256] = block[64:128]
            in_term = dot(hid_t[...], mix[:, 128:256]).astype(BF)
            for s in range(SEQ):
                terms[0, s, :, 0:128] = in_term[64 * s : 64 * s + 64]
        else:
            in_term = dot(hid_t[...], mix[:, 256:512]).astype(BF)
            for s in range(SEQ):
                terms[1, s] = in_term[64 * s : 64 * s + 64]
        for h in range(4):
            for k in NEAR:
                sends.append(
                    push(
                        terms.at[n, 4 * h + lax.rem(y + k, YS)], from_y.at[n, y, h],
                        y_s.at[n, k, h], y_r.at[n, y, h], (dp, at_y(k)),
                    )
                )

    def along_z(n):
        for k in (1, 2, 3, 0):
            h = lax.rem(zh + k, 4)
            total = terms[n, 4 * h + y].astype(F32)
            for m in NEAR:
                t = lax.rem(y + m, YS)
                arrival(from_y.at[n, t, h], y_r.at[n, t, h], (dp, at_y(m)))
                total += from_y[n, t, h].astype(F32)
            to_z[n, h] = total.astype(BF)
            if k:
                sends.append(
                    push(
                        to_z.at[n, h], from_z.at[n, zh], z_s.at[n, h], z_r.at[n, zh],
                        (dp, h * YS + y),
                    )
                )

    def across(n):
        total = to_z[n, zh].astype(F32)
        for k in NEAR:
            h = lax.rem(zh + k, 4)
            arrival(from_z.at[n, h], z_r.at[n, h], (dp, at_z(k)))
            total += from_z[n, h].astype(F32)
        from_z[n, zh] = total.astype(BF)
        sends.append(push(from_z.at[n, zh], from_zl.at[n], zl_s.at[n], zl_r.at[n], partner))

    def to_team(n):
        arrival(from_zl.at[n], zl_r.at[n], partner)
        full[n, me] = (from_z[n, zh].astype(F32) + from_zl[n].astype(F32)).astype(BF)
        for k in range(1, TEAM):
            sends.append(
                push(
                    full.at[n, me], full.at[n, me], g_s.at[n, k], g_r.at[n, me], (team_peer(k), r)
                )
            )

    def from_team(n):
        for k in range(1, TEAM):
            i = lax.rem(p + k, TEAM)
            q = slot_of(i)
            arrival(full.at[n, q], g_r.at[n, q], (base + i, r))

    def out_piece(i):
        t = 2 * i + r % 2
        src = full.at[0, (i % 2) * XS + i // 2, :, 128:256]
        return t, remote(src, wob.at[r // 2], q_s.at[i], q_r.at[r // 2], (dp, t))

    for core in (1 - c, c):
        take(core, 0)
        if core is not c:
            share(0)
    terms_out(0)
    pass_on(0)
    along_z(0)
    take(1 - c, 1)
    take(c, 1)
    terms_out(1)
    share(1)
    across(0)
    pass_on(1)
    to_team(0)
    along_z(1)
    layer_out[...] = result_of(0, hid8[me])
    from_team(0)
    for i in range(TEAM):
        t, copy = out_piece(i)

        @pl.when(t != r)
        def _():
            copy.start()

        @pl.when(t == r)
        def _():
            wob[r // 2] = full[0, (i % 2) * XS + i // 2, :, 128:256]

    across(1)
    for i in range(TEAM):
        q = (i % 2) * XS + i // 2
        proj_grad[:, 0, 128 * i : 128 * i + 128] = full[0, q, :, 0:128].astype(F32)
    to_team(1)
    for j in range(TEAM):
        t, copy = out_piece(j)

        @pl.when(t != r)
        def _():
            arrival(wob.at[j], q_r.at[j], (dp, t))
            copy.wait_send()

        proj_grad[:, 3, 128 * j : 128 * j + 128] = wob[j].astype(F32)
    features_grad[...] = result_of(1, cot8[me])
    from_team(1)
    for i in range(TEAM):
        q = (i % 2) * XS + i // 2
        proj_grad[:, 1, 128 * i : 128 * i + 128] = full[1, q, :, 0:128].astype(F32)
        proj_grad[:, 2, 128 * i : 128 * i + 128] = full[1, q, :, 128:256].astype(F32)

    for copy in sends:
        copy.wait_send()

    @pl.when(spread)
    def _():
        for j in range(TEAM):
            t = 2 * j + r % 2

            @pl.when(t != r)
            def _():
                remote(
                    wt.at[j, :, 384:512], out_part(t), sc_s.at[j], sc_r, (dp, t)
                ).wait_send()

    def sent(k, carry):
        t = lax.rem(r + k, SEQ)
        for half in (0, 1):
            remote(
                stage.at[t, half], land[half].at[r], a_s.at[t, half], a_r.at[r, half], (dp, t)
            ).wait_send()
            remote(
                back.at[t, half], home.at[r, half], b_s.at[t, half], b_r.at[r, half], (dp, t)
            ).wait_send()
        return carry

    lax.fori_loop(1, SEQ, sent, 0)


def layer(hid, cot, wt, tab):
    vmem = pl.BlockSpec(memory_space=pltpu.VMEM)
    dma = pltpu.SemaphoreType.DMA
    tile = (128, 128)
    act = (ROWS, WIDTH)
    return pl.pallas_call(
        kernel,
        out_shape=[
            jax.ShapeDtypeStruct(act, BF),
            jax.ShapeDtypeStruct(act, BF),
            jax.ShapeDtypeStruct((SHARD, 4, WIDTH), F32),
        ],
        in_specs=[vmem] * 4,
        out_specs=[vmem] * 3,
        scratch_shapes=[
            pltpu.VMEM((TEAM, *act), BF),
            pltpu.VMEM((TEAM, *act), BF),
            pltpu.VMEM((WIDTH, TEAM * ROWS), BF),
            pltpu.VMEM((WIDTH, 512), BF),
            pltpu.VMEM((WIDTH, 128), BF),
            pltpu.VMEM((512, WIDTH), BF),
            pltpu.VMEM((TEAM, 8, 128), jnp.int32),
            pltpu.SMEM((8, 128), jnp.int32),
            pltpu.VMEM((SEQ, 2, *tile), BF),
            pltpu.VMEM((SEQ, *tile), BF),
            pltpu.VMEM((SEQ, *tile), BF),
            pltpu.VMEM((SEQ, 4, *tile), F32),
            pltpu.VMEM((SEQ * 4 + 1, *tile), F32),
            pltpu.VMEM((SEQ, 2, *tile), BF),
            pltpu.VMEM((SEQ, 2, *tile), BF),
            pltpu.VMEM((TEAM * ROWS, 512), BF),
            pltpu.VMEM((2, 2 * XS, *act), BF),
            pltpu.VMEM((2, XS, *act), BF),
            pltpu.VMEM((2, XS, *act), BF),
            pltpu.VMEM((2, SEQ, SHARD, 256), BF),
            pltpu.VMEM((2, YS, 4, SHARD, 256), BF),
            pltpu.VMEM((2, 4, SHARD, 256), BF),
            pltpu.VMEM((2, 4, SHARD, 256), BF),
            pltpu.VMEM((2, SHARD, 256), BF),
            pltpu.VMEM((2, TEAM, SHARD, 256), BF),
            pltpu.VMEM((TEAM, SHARD, 128), BF),
            dma((8,)), dma((8,)), dma((8,)), dma((8,)), dma((8,)), dma((8,)),
            dma((17,)), dma((16,)), dma((17,)), dma((16,)), dma((17,)), dma((16,)), dma((8,)), dma(()),
            dma((16, 2)), dma((16, 2)), dma((16, 2)), dma((16, 2)),
            dma((2,)), dma((2,)), dma((2, 4)), dma((2, 4)), dma((2, 4, 4)), dma((2, 4, 4)),
            dma((2, 4)), dma((2, 4)), dma((2,)), dma((2,)), dma((2, 8)), dma((2, 8)),
            dma((8,)), dma((8,)), dma((4,)),
        ],
        compiler_params=pltpu.CompilerParams(
            collective_id=1, has_side_effects=True, vmem_limit_bytes=VMEM_BYTES
        ),
    )(hid, cot, wt, tab)


def tables(order, neigh, count):
    spots = lax.iota(jnp.int32, SEQ)
    listing = 4 * spots[:, None] + lax.iota(jnp.int32, 4)[None, :]
    named = neigh[None] == order[:, None, None]
    users = jnp.min(jnp.where(named, listing[None], 64), axis=2)
    slots = jnp.sum(jnp.where(named, spots[:, None, None], 0), axis=0)
    flat = jnp.concatenate([users.reshape(-1), slots.reshape(-1), count, jnp.zeros((48,), jnp.int32)])
    return jnp.concatenate([flat.reshape(3, 128), jnp.zeros((5, 128), jnp.int32)])


def per_device(
    features, labels, label_table, proj_weight, block_order, neighbours, counts, cotangent
):
    onehot = (labels[0][:, None] == lax.iota(jnp.int32, label_table.shape[0])[None, :]).astype(BF)
    hidden = (
        features[0].astype(F32) + jnp.dot(onehot, label_table, preferred_element_type=F32)
    ).astype(BF)
    wt = proj_weight.reshape(SHARD, 4, TEAM, 128).transpose(2, 0, 1, 3).reshape(TEAM, SHARD, 512)
    tab = tables(block_order[0], neighbours[0], counts[0])
    layer_out, features_grad, proj_grad = layer(hidden, cotangent[0], wt, tab)
    return (layer_out[None], features_grad[None], proj_grad)


def solution(mesh):
    placed = (
        P("dp", "seq", None),
        P("dp", "seq"),
        P(),
        P("seq", None, None),
        P("dp", None),
        P("dp", None, None),
        P("dp", None),
        P("dp", "seq", None),
    )
    return jax.shard_map(
        per_device,
        mesh=mesh,
        in_specs=placed,
        out_specs=(P("dp", "seq", None), P("dp", "seq", None), P("seq", None, None)),
        check_vma=False,
    )
```

time: 554 us -> 133 us (0.24)
  waiting for transfers between devices: 380 us -> 0 us
  Pallas kernels: 0 us -> 125 us
  matrix products: 55.4 us -> 1.32 us
  local copies, waits for them, and re-layouts: 53 us -> 5.76 us
  starting transfers between devices: 37.8 us -> 0 us
  between operations: 14 us -> 0.74 us
  other arithmetic: 12.6 us -> 0.17 us
    pallas_call x0 -> x1, Pallas kernels: none -> 125 us  [layer(): pl.pallas_call(kernel, out_shape=[jax.ShapeDtypeStruct(act, BF), jax.Shap...]
    reduce_scatter x1 -> x0, waiting for transfers between devices: 119 us -> none  [per_device(): lax.psum_scatter(jnp.concatenate([lax.dot_general(hidden, grad_qkv, contr...]
    all_gather x1 -> x0, waiting for transfers between devices: 116 us -> none  [per_device(): weights = lax.all_gather(proj_weight, 'seq', axis=0, tiled=True)]
    psum x1 -> x0, waiting for transfers between devices: 115 us -> none  [per_device(): lax.psum(lax.psum_scatter(jnp.concatenate([lax.dot_general(hidden, grad_q...]
    dot_general x43 -> x1, matrix products: 55.4 us -> 1.32 us  [per_device(): jnp.dot(onehot, label_table, preferred_element_type=F32)]
    all_to_all x4 -> x0, starting transfers between devices: 37.6 us -> none  [the longest x1 12 us: per_device(): lax.all_to_all(qkv, 'seq', split_axis=2, concat_axis=0, tiled=True)]
    all_to_all x4 -> x0, waiting for transfers between devices: 28.7 us -> none  [the longest x1 18.8 us: per_device(): lax.all_to_all(stacked, 'seq', split_axis=0, concat_axis=2, tiled=True)]
    unnamed x28 -> x15, local copies, waits for them, and re-layouts: 20.2 us -> 5.12 us
  transfers between devices with their start and end apart: 7 -> 0, of which waited for: 5 -> 0; matrix products, arithmetic and copies ran while one was open for 16% -> 0% of each run, Pallas kernels for 0% -> 0%
where the time goes in v2:
time: 133 us
  Pallas kernels  125 us (94%)
  local copies, waits for them, and re-layouts  5.76 us (4%)
    pallas_call x1, Pallas kernels, layer(): pl.pallas_call(kernel, out_shape=[jax.ShapeDtypeStruct(act, BF), jax.Shap...  125 us
    unnamed x15, local copies, waits for them, and re-layouts  5.12 us

profile of v2, /device:TPU:1, one launch (start us, length us, event | category | flops | bytes accessed | tf_op | source)
XLA Modules:
  0.0 132.9 jit_solution(11582208491127626239)
XLA Ops:
  0.6 0.0 copy-start
  0.6 0.0 copy-start.2
  0.7 0.0 copy-start.5
  0.7 0.7 copy-done.2
  1.4 0.0 copy-done.5
  1.4 0.1 fusion.2
  1.5 0.1 reshape.51
  1.6 0.1 copy.16
  1.6 0.1 reshape.52
  1.7 0.0 copy-start.4
  1.8 0.6 copy-done.4
  2.4 0.1 add_bitcast_fusion
  2.5 0.0 copy-start.3
  2.5 0.6 copy-done.3
  3.1 1.3 fusion.hid
  4.5 0.0 copy-done
  4.5 0.2 bitcast_bitcast_fusion
  4.7 0.0 copy-start.1
  4.7 0.2 reshape.50.wt
  4.9 0.7 copy-done.1
  5.6 124.9 %shard_map.103 = (bf16[128,1024]{1,0:T(8,128)(2,1)S(1)}, bf16[128,1024]{1,0:T(8,128)(2,1)S(1)}, f32[64,4,1024]{2,1,0:T(4,128)S(1)}) custom-call(bf16[128,1024]{1,0:T(8,128)(2,1)S(1)} %fusion.hid, bf16[128,1024]{1,0:T(8,128)(2,1)S(1)} %bitcast.22, bf16[8,64,512]{2,1,0:T(8,128)(2,1)S(1)} %reshape.50.wt, s32[8,128]{1,0:T(8,128)S(1)} %concatenate.7.tab), custom_call_target="tpu_custom_call" | custom-call | tf_op jit(solution)/shard_map/pallas_call | solution.py:564
  130.5 0.7 copy.22
  131.2 0.7 copy.23
  131.9 1.0 copy.24
  (4 shorter events, 0.0 us)
Async XLA Ops:
  0.6 3.8 %copy-start = (bf16[64,4,1024]{2,1,0:T(4,128)(2,1)S(1)}, bf16[64,4,1024]{2,1,0:T(4,128)(2,1)}, u32[]{:S(2)}) copy-start(bf16[64,4,1024]{2,1,0:T(4,128)(2,1)} %param.11) | copy-start | bytes 1572868
  0.6 0.7 copy-start.2
  0.7 0.7 copy-start.5
  1.7 0.7 copy-start.4
  2.5 0.7 copy-start.3
  4.7 1.0 copy-start.1

commit v3 on v2

--- a/solution.py
+++ b/solution.py
@@ -52,10 +52,11 @@
 def kernel(
     hid, cot, wt, tab,
     layer_out, features_grad, proj_grad,
-    hid8, cot8, hid_t, wg, wo, w_t, tab8, tabs, stage, land_qk, land_vg, probs, tiles, back, home, mix,
-    part, sib, far, terms, from_y, to_z, from_z, from_zl, full, wob,
-    hid_s, hid_r, cot_s, cot_r, tab_s, tab_r, w_s, w_r, v_s, v_r, o_s, o_r, sc_s, sc_r, a_s, a_r, b_s, b_r,
-    sib_s, sib_r, far_s, far_r, y_s, y_r, z_s, z_r, zl_s, zl_r, g_s, g_r, q_s, q_r, loc,
+    hid8, cot8, hid_t, wg, wo, w_t, tab8, tabs, stage_qk, stage_v, stage_g, land_qk, land_v, land_g,
+    v_full, probs, lows, tiles, back_a, back_q, back_kv, home_a, home_q, home_kv, mix,
+    part, total, sib, far, terms, from_y, to_z, from_z, from_zl, full, wob,
+    hid_s, hid_r, hid_h, cot_s, cot_r, cot_h, tab_s, tab_r, w_s, w_r, v_s, v_r, o_s, o_r, sc_s, sc_r,
+    m_s, m_r, sib_s, sib_r, far_s, far_r, y_s, y_r, z_s, z_r, zl_s, zl_r, g_s, g_r, q_s, q_r, loc,
 ):
     dp, r = lax.axis_index("dp"), lax.axis_index("seq")
     zl, p = dp // TEAM, dp % TEAM
@@ -94,7 +95,63 @@
         pl.semaphore_signal(barrier, inc=1, device_id=where, device_id_type=MESH)
     pl.semaphore_wait(barrier, len(greeted))
     sends = []
-    land = (land_qk, land_vg)
+
+    sources = (stage_qk, stage_v, stage_g, back_a, back_q, back_kv)
+    targets = (land_qk, land_v, land_g, home_a, home_q, home_kv)
+
+    def message(kind, t):
+        return remote(
+            sources[kind].at[t], targets[kind].at[r], m_s.at[kind, t], m_r.at[kind, r], (dp, t)
+        )
+
+    def give(kind, t):
+        @pl.when(t != r)
+        def _():
+            message(kind, t).start()
+
+        @pl.when(t == r)
+        def _():
+            targets[kind][r] = sources[kind][t]
+
+    def got(kind, t):
+        @pl.when(t != r)
+        def _():
+            arrival(targets[kind].at[t], m_r.at[kind, t], (dp, t))
+
+    def got_all(kind):
+        def one(k, carry):
+            t = lax.rem(r + k, SEQ)
+            arrival(targets[kind].at[t], m_r.at[kind, t], (dp, t))
+            return carry
+
+        lax.fori_loop(1, SEQ, one, 0)
+
+    halves = (pl.ds(0, 64), pl.ds(64, 64))
+
+    def spread_x(array, own, send, recv):
+        for k in (1, 3):
+            sends.append(push(own, array.at[me], send.at[k], recv.at[me], at_x(k)))
+        sends.append(push(own, array.at[me], send.at[0], recv.at[me], sibling))
+
+    def forward_x(array, send, recv, opposite):
+        for k in (1, 3):
+            q = slot(k)
+            arrival(array.at[q], recv.at[q], at_x(k))
+            h = k // 3
+            piece = array.at[q, halves[h]]
+            sends.append(push(piece, piece, send.at[4 + k], opposite.at[h], at_x(4 - k)))
+            sends.append(push(array.at[q], array.at[q], send.at[1 + k], recv.at[q], sibling))
+
+    def finish_x(array, send, recv, opposite):
+        q = slot(2)
+        for h, k in ((0, 1), (1, 3)):
+            arrival(array.at[q, halves[h]], opposite.at[h], at_x(k))
+        sends.append(push(array.at[q], array.at[q], send.at[6], recv.at[q], sibling))
+
+    def other_core(array, recv):
+        for k in range(XS):
+            q = (1 - c) * XS + turn(k)
+            arrival(array.at[q], recv.at[q], sibling)
 
     def rows_of(s):
         return pl.ds(pl.multiple_of(s * SHARD, SHARD), SHARD)
@@ -133,9 +190,7 @@
     keep_hid.start()
     keep_cot = pltpu.make_async_copy(cot, cot8.at[me], loc.at[2])
     keep_cot.start()
-    for k in NEAR:
-        sends.append(push(hid, hid8.at[me], hid_s.at[k], hid_r.at[me], at_x(k)))
-    sends.append(push(hid, hid8.at[me], hid_s.at[0], hid_r.at[me], sibling))
+    spread_x(hid8, hid, hid_s, hid_r)
     for k in range(1, TEAM):
         sends.append(push(tab, tab8.at[me], tab_s.at[k], tab_r.at[me], (team_peer(k), r)))
 
@@ -153,6 +208,9 @@
                 push(v_part(s), v_part(s), v_s.at[7 + n * 3 + m], v_r.at[s], (dp, at_z(m)))
             )
 
+    forward_x(hid8, hid_s, hid_r, hid_h)
+    spread_x(cot8, cot, cot_s, cot_r)
+
     piece = out_part(r)
 
     @pl.when(spread)
@@ -169,14 +227,7 @@
         sends.append(push(piece, piece, o_s.at[k], o_r.at[r], (dp, at_z(k))))
     for k in NEAR:
         sends.append(push(piece, piece, o_s.at[3 + k], o_r.at[r], (dp, at_y(k))))
-
-    for n, k in enumerate(NEAR):
-        q = slot(k)
-        arrival(hid8.at[q], hid_r.at[q], at_x(k))
-        sends.append(push(hid8.at[q], hid8.at[q], hid_s.at[4 + n], hid_r.at[q], sibling))
-    for k in NEAR:
-        sends.append(push(cot, cot8.at[me], cot_s.at[k], cot_r.at[me], at_x(k)))
-    sends.append(push(cot, cot8.at[me], cot_s.at[0], cot_r.at[me], sibling))
+    finish_x(hid8, hid_s, hid_r, hid_h)
     for n, k in enumerate(NEAR):
         s = at_z(k)
         arrival(out_part(s), o_r.at[s], (dp, s))
@@ -191,45 +242,37 @@
                 s = lax.rem(zh + k, 4) * YS + lax.rem(y + m, YS)
                 arrival(piece_of(s), sems.at[s], (dp, s))
 
+    def group_rows(array, core):
+        block = array[pl.ds(pl.multiple_of(core * XS, XS), XS)]
+        return block.reshape(HALF, array.shape[2])
+
+    def packed(stage, kind, core, result):
+        for n in range(XS):
+            top = result[n * ROWS : n * ROWS + 64]
+            bottom = result[n * ROWS + 64 : n * ROWS + ROWS]
+            i = core * XS + n
+            stage[2 * i] = merge(top, bottom)
+            stage[2 * i + 1] = merge_high(top, bottom)
+            give(kind, 2 * i)
+            give(kind, 2 * i + 1)
+
     from_all_y(qk_part, w_r)
     own_w.wait()
     keep_hid.wait()
-
-    def deliver(t, half):
-        @pl.when(t != r)
-        def _():
-            push(
-                stage.at[t, half], land[half].at[r], a_s.at[t, half], a_r.at[r, half], (dp, t)
-            )
-
-        @pl.when(t == r)
-        def _():
-            land[half][r] = stage[t, half]
-
-    def group_rows(array, core):
-        block = array[pl.ds(pl.multiple_of(core * XS, XS), XS)]
-        return block.reshape(HALF, array.shape[2])
-
     for core in (c, 1 - c):
         if core is not c:
-            for k in range(XS):
-                q = (1 - c) * XS + turn(k)
-                arrival(hid8.at[q], hid_r.at[q], sibling)
+            other_core(hid8, hid_r)
         queries_keys = dot(group_rows(hid8, core), wg[:, 0:256]).astype(BF)
         for n in range(XS):
             rows = queries_keys[n * ROWS : n * ROWS + ROWS]
             q, k = rows[:, 0:128], rows[:, 128:256]
             i = core * XS + n
-            stage[2 * i, 0] = merge(q, k)
-            stage[2 * i + 1, 0] = merge_high(q, k)
-            deliver(2 * i, 0)
-            deliver(2 * i + 1, 0)
-
-    keep_cot.wait()
-    for n, k in enumerate(NEAR):
-        q = slot(k)
-        arrival(cot8.at[q], cot_r.at[q], at_x(k))
-        sends.append(push(cot8.at[q], cot8.at[q], cot_s.at[4 + n], cot_r.at[q], sibling))
+            stage_qk[2 * i] = merge(q, k)
+            stage_qk[2 * i + 1] = merge_high(q, k)
+            give(0, 2 * i)
+            give(0, 2 * i + 1)
+
+    forward_x(cot8, cot_s, cot_r, cot_h)
     for m in NEAR:
         for k in range(1, 4):
             s = lax.rem(zh + k, 4) * YS + lax.rem(y + m, YS)
@@ -237,26 +280,19 @@
     for k in NEAR:
         s = at_z(k)
         arrival(v_part(s), v_r.at[s], (dp, s))
+    for core in (c, 1 - c):
+        packed(stage_v, 1, core, dot(group_rows(hid8, core), wg[:, 256:384]).astype(BF))
     from_all_y(out_part, o_r)
     for j in range(TEAM):
         block = wg[128 * j : 128 * j + 128, 384:512]
         wo[128 * j : 128 * j + 128, :] = block.T
         w_t[384:512, 128 * j : 128 * j + 128] = block
+    finish_x(cot8, cot_s, cot_r, cot_h)
+    keep_cot.wait()
     for core in (c, 1 - c):
         if core is not c:
-            for k in range(XS):
-                q = (1 - c) * XS + turn(k)
-                arrival(cot8.at[q], cot_r.at[q], sibling)
-        values = dot(group_rows(hid8, core), wg[:, 256:384]).astype(BF)
-        grad = dot(group_rows(cot8, core), wo[...]).astype(BF)
-        for n in range(XS):
-            g = grad[n * ROWS : n * ROWS + ROWS]
-            v = values[n * ROWS : n * ROWS + ROWS]
-            i = core * XS + n
-            stage[2 * i, 1] = merge(v, g)
-            stage[2 * i + 1, 1] = merge_high(v, g)
-            deliver(2 * i, 1)
-            deliver(2 * i + 1, 1)
+            other_core(cot8, cot_r)
+        packed(stage_g, 2, core, dot(group_rows(cot8, core), wo[...]).astype(BF))
 
     for n in range(3):
         w_t[128 * n : 128 * n + 128, :] = wg[:, 128 * n : 128 * n + 128].T
@@ -272,17 +308,9 @@
     to_scalars.start()
     to_scalars.wait()
 
-    def all_landed(half):
-        def one(k, carry):
-            t = lax.rem(r + k, SEQ)
-            arrival(land[half].at[t], a_r.at[t, half], (dp, t))
-            return carry
-
-        lax.fori_loop(1, SEQ, one, 0)
-
     lo = low_lanes((128, 128))
     zero = jnp.zeros((128, 128), BF)
-    all_landed(0)
+    got_all(0)
 
     def probabilities(s):
         qz = jnp.where(lo, zero, pltpu.roll(land_qk[s], 64, 1)) * jnp.asarray(0.125, BF)
@@ -299,7 +327,9 @@
         total = jnp.sum((expo[0] + expo[1]) + (expo[2] + expo[3]), axis=0, keepdims=True)
         inv = 1.0 / total
         for j in range(4):
-            probs[s, j] = expo[j] * inv
+            prob = expo[j] * inv
+            probs[s, j] = prob
+            lows[s, 128 * j : 128 * j + 128] = prob.astype(BF)
 
     def forward(g, carry):
         for n in range(4):
@@ -307,42 +337,52 @@
         return carry
 
     lax.fori_loop(0, 4, forward, 0)
-    all_landed(1)
-
-    def give_back(s, half):
-        @pl.when(s != r)
-        def _():
-            push(back.at[s, half], home.at[r, half], b_s.at[s, half], b_r.at[r, half], (dp, s))
-
-        @pl.when(s == r)
-        def _():
-            home[r, half] = back[s, half]
+    got_all(1)
+    for s in range(SEQ):
+        v_full[s, 0:64] = land_v[s]
+        v_full[s, 64:128] = pltpu.roll(land_v[s], 64, 1)
+
+    def blocks_of(g):
+        return [lax.rem(r + 1 + 4 * g + n, SEQ) for n in range(4)]
+
+    def attention(g, carry):
+        for s in blocks_of(g):
+            values = [v_full[tabs[2, 4 * s + j]] for j in range(4)]
+            attn = dot(jnp.concatenate(values, axis=0), lows[s], TN).T.astype(BF)
+            back_a[s] = merge(attn[0:64], attn[64:128])
+        for s in blocks_of(g):
+            give(3, s)
+        return carry
+
+    lax.fori_loop(0, 4, attention, 0)
+    got_all(2)
 
     def gradients(s):
-        qk, vg = land_qk[s], land_vg[s]
-        gz = jnp.where(lo, pltpu.roll(vg, 64, 1), zero)
-        rhs = jnp.concatenate([jnp.where(lo, qk, zero), jnp.where(lo, zero, vg)], axis=0)
+        qk, grad = land_qk[s], land_g[s]
+        turned = pltpu.roll(grad, 64, 1)
+        gz = jnp.where(lo, jnp.concatenate([grad, turned], axis=0), zero)
+        gv = jnp.where(lo, zero, jnp.concatenate([turned, grad], axis=0))
+        rhs = jnp.concatenate([jnp.where(lo, qk, zero), gv], axis=0)
         slots = [tabs[2, 4 * s + j] for j in range(4)]
         keys = [land_qk[b] for b in slots]
-        values = [land_vg[b] for b in slots]
-        grad_p = [dot(v, gz, NT) for v in values]
+        grad_p = [dot(v_full[b], gz, NT) for b in slots]
         prob = [probs[s, j] for j in range(4)]
         prod = [a * g for a, g in zip(prob, grad_p)]
         delta = jnp.sum((prod[0] + prod[1]) + (prod[2] + prod[3]), axis=0, keepdims=True)
-        low = [a.astype(BF) for a in prob]
         grad_s = [(a * (g - delta) * 0.125).astype(BF) for a, g in zip(prob, grad_p)]
-        attn = dot(jnp.concatenate(values, axis=0), jnp.concatenate(low, axis=0), TN)
-        grad_q = dot(jnp.concatenate(keys, axis=0), jnp.concatenate(grad_s, axis=0), TN)
-        back[s, 0] = jnp.concatenate([attn[0:64], grad_q[64:128]], axis=0).T.astype(BF)
+        grad_q = dot(
+            jnp.concatenate(keys, axis=0), jnp.concatenate(grad_s, axis=0), TN
+        ).T.astype(BF)
+        back_q[s] = merge_high(grad_q[0:64], grad_q[64:128])
         for j in range(4):
-            tiles[4 * s + j] = dot(jnp.concatenate([grad_s[j], low[j]], axis=1), rhs)
+            low = lows[s, 128 * j : 128 * j + 128]
+            tiles[4 * s + j] = dot(jnp.concatenate([grad_s[j], low], axis=1), rhs)
 
     def backward(g, carry):
-        blocks = [lax.rem(r + 1 + 4 * g + n, SEQ) for n in range(4)]
-        for s in blocks:
+        for s in blocks_of(g):
             gradients(s)
-        for s in blocks:
-            give_back(s, 0)
+        for s in blocks_of(g):
+            give(4, s)
         return carry
 
     lax.fori_loop(0, 4, backward, 0)
@@ -353,29 +393,29 @@
         total = tiles[tabs[b // 8, (b % 8) * 16]]
         for s in range(1, SEQ):
             total += tiles[tabs[b // 8, (b % 8) * 16 + s]]
-        back[b, 1] = total.astype(BF)
-        give_back(b, 1)
+        back_kv[b] = total.astype(BF)
+        give(5, b)
         return carry
 
     lax.fori_loop(0, SEQ, collect, 0)
-
-    def came_home(t, half):
-        @pl.when(t != r)
-        def _():
-            arrival(home.at[t, half], b_r.at[t, half], (dp, t))
 
     def half_rows(core):
         return pl.ds(pl.multiple_of(core * HALF, HALF), HALF)
 
-    def take(core, half):
+    def take(core, kind):
         for n in range(XS):
             i = core * XS + n
-            came_home(2 * i, half)
-            came_home(2 * i + 1, half)
-            a, b = home[2 * i, half], home[2 * i + 1, half]
-            rows = pl.ds(pl.multiple_of(i * ROWS, ROWS), ROWS)
-            mix[rows, 256 * half : 256 * half + 128] = merge(a, b)
-            mix[rows, 256 * half + 128 : 256 * half + 256] = merge_high(a, b)
+            got(kind, 2 * i)
+            got(kind, 2 * i + 1)
+            a, b = targets[kind][2 * i], targets[kind][2 * i + 1]
+            start = pl.multiple_of(i * ROWS, ROWS)
+            if kind == 5:
+                mix[pl.ds(start, ROWS), 256:384] = merge(a, b)
+                mix[pl.ds(start, ROWS), 384:512] = merge_high(a, b)
+            else:
+                cols = pl.ds(128 * (kind - 3), 128)
+                mix[pl.ds(start, 64), cols] = merge(a, b)
+                mix[pl.ds(start + 64, 64), cols] = merge_high(a, b)
 
     def product(core, n):
         if n == 0:
@@ -386,27 +426,29 @@
         result = product(1 - c, n).astype(BF)
         for i in range(XS):
             part[n, i] = result[i * ROWS : i * ROWS + ROWS]
-        sends.append(push(part.at[n, 0:XS], sib.at[n], sib_s.at[n], sib_r.at[n], sibling))
+        for k in (1, 3, 2, 0):
+            i = turn(k)
+            sends.append(push(part.at[n, i], sib.at[n, i], sib_s.at[n, k], sib_r.at[n, i], sibling))
 
     def pass_on(n):
         result = product(c, n)
-        arrival(sib.at[n], sib_r.at[n], sibling)
         for i in range(XS):
-            total = result[i * ROWS : i * ROWS + ROWS] + sib[n, i].astype(F32)
-            part[n, XS + i] = total.astype(BF)
-        for k in NEAR:
-            sends.append(
-                push(
-                    part.at[n, XS + turn(k)], far.at[n, x], far_s.at[n, k], far_r.at[n, x], at_x(k)
+            total[i] = result[i * ROWS : i * ROWS + ROWS]
+        for k in (1, 3, 2, 0):
+            i = turn(k)
+            arrival(sib.at[n, i], sib_r.at[n, i], sibling)
+            part[n, XS + i] = (total[i] + sib[n, i].astype(F32)).astype(BF)
+            if k:
+                sends.append(
+                    push(part.at[n, XS + i], far.at[n, x], far_s.at[n, k], far_r.at[n, x], at_x(k))
                 )
-            )
 
     def result_of(n, first):
-        total = first.astype(F32) + part[n, XS + x].astype(F32)
+        result = first.astype(F32) + part[n, XS + x].astype(F32)
         for k in NEAR:
             arrival(far.at[n, turn(k)], far_r.at[n, turn(k)], at_x(k))
-            total += far[n, turn(k)].astype(F32)
-        return total.astype(BF)
+            result += far[n, turn(k)].astype(F32)
+        return result.astype(BF)
 
     def terms_out(n):
         if n == 0:
@@ -419,11 +461,11 @@
             in_term = dot(hid_t[...], mix[:, 128:256]).astype(BF)
             for s in range(SEQ):
                 terms[0, s, :, 0:128] = in_term[64 * s : 64 * s + 64]
-        else:
-            in_term = dot(hid_t[...], mix[:, 256:512]).astype(BF)
-            for s in range(SEQ):
-                terms[1, s] = in_term[64 * s : 64 * s + 64]
         for h in range(4):
+            if n == 1:
+                in_term = dot(hid_t[256 * h : 256 * h + 256], mix[:, 256:512]).astype(BF)
+                for m in range(YS):
+                    terms[1, 4 * h + m] = in_term[64 * m : 64 * m + 64]
             for k in NEAR:
                 sends.append(
                     push(
@@ -479,19 +521,20 @@
         src = full.at[0, (i % 2) * XS + i // 2, :, 128:256]
         return t, remote(src, wob.at[r // 2], q_s.at[i], q_r.at[r // 2], (dp, t))
 
-    for core in (1 - c, c):
-        take(core, 0)
-        if core is not c:
-            share(0)
+    take(1 - c, 3)
+    share(0)
+    take(c, 3)
+    pass_on(0)
+    take(1 - c, 4)
+    take(c, 4)
     terms_out(0)
-    pass_on(0)
-    along_z(0)
-    take(1 - c, 1)
-    take(c, 1)
+    take(1 - c, 5)
+    take(c, 5)
     terms_out(1)
     share(1)
+    along_z(0)
+    pass_on(1)
     across(0)
-    pass_on(1)
     to_team(0)
     along_z(1)
     layer_out[...] = result_of(0, hid8[me])
@@ -544,13 +587,8 @@
 
     def sent(k, carry):
         t = lax.rem(r + k, SEQ)
-        for half in (0, 1):
-            remote(
-                stage.at[t, half], land[half].at[r], a_s.at[t, half], a_r.at[r, half], (dp, t)
-            ).wait_send()
-            remote(
-                back.at[t, half], home.at[r, half], b_s.at[t, half], b_r.at[r, half], (dp, t)
-            ).wait_send()
+        for kind in range(6):
+            message(kind, t).wait_send()
         return carry
 
     lax.fori_loop(1, SEQ, sent, 0)
@@ -559,7 +597,7 @@
 def layer(hid, cot, wt, tab):
     vmem = pl.BlockSpec(memory_space=pltpu.VMEM)
     dma = pltpu.SemaphoreType.DMA
-    tile = (128, 128)
+    tile, small = (128, 128), (64, 128)
     act = (ROWS, WIDTH)
     return pl.pallas_call(
         kernel,
@@ -579,15 +617,25 @@
             pltpu.VMEM((512, WIDTH), BF),
             pltpu.VMEM((TEAM, 8, 128), jnp.int32),
             pltpu.SMEM((8, 128), jnp.int32),
-            pltpu.VMEM((SEQ, 2, *tile), BF),
             pltpu.VMEM((SEQ, *tile), BF),
+            pltpu.VMEM((SEQ, *small), BF),
+            pltpu.VMEM((SEQ, *small), BF),
+            pltpu.VMEM((SEQ, *tile), BF),
+            pltpu.VMEM((SEQ, *small), BF),
+            pltpu.VMEM((SEQ, *small), BF),
             pltpu.VMEM((SEQ, *tile), BF),
             pltpu.VMEM((SEQ, 4, *tile), F32),
+            pltpu.VMEM((SEQ, 512, 128), BF),
             pltpu.VMEM((SEQ * 4 + 1, *tile), F32),
-            pltpu.VMEM((SEQ, 2, *tile), BF),
-            pltpu.VMEM((SEQ, 2, *tile), BF),
+            pltpu.VMEM((SEQ, *small), BF),
+            pltpu.VMEM((SEQ, *small), BF),
+            pltpu.VMEM((SEQ, *tile), BF),
+            pltpu.VMEM((SEQ, *small), BF),
+            pltpu.VMEM((SEQ, *small), BF),
+            pltpu.VMEM((SEQ, *tile), BF),
             pltpu.VMEM((TEAM * ROWS, 512), BF),
             pltpu.VMEM((2, 2 * XS, *act), BF),
+            pltpu.VMEM((XS, *act), F32),
             pltpu.VMEM((2, XS, *act), BF),
             pltpu.VMEM((2, XS, *act), BF),
             pltpu.VMEM((2, SEQ, SHARD, 256), BF),
@@ -597,10 +645,10 @@
             pltpu.VMEM((2, SHARD, 256), BF),
             pltpu.VMEM((2, TEAM, SHARD, 256), BF),
             pltpu.VMEM((TEAM, SHARD, 128), BF),
-            dma((8,)), dma((8,)), dma((8,)), dma((8,)), dma((8,)), dma((8,)),
+            dma((8,)), dma((8,)), dma((2,)), dma((8,)), dma((8,)), dma((2,)), dma((8,)), dma((8,)),
             dma((17,)), dma((16,)), dma((17,)), dma((16,)), dma((17,)), dma((16,)), dma((8,)), dma(()),
-            dma((16, 2)), dma((16, 2)), dma((16, 2)), dma((16, 2)),
-            dma((2,)), dma((2,)), dma((2, 4)), dma((2, 4)), dma((2, 4, 4)), dma((2, 4, 4)),
+            dma((6, 16)), dma((6, 16)),
+            dma((2, 4)), dma((2, 4)), dma((2, 4)), dma((2, 4)), dma((2, 4, 4)), dma((2, 4, 4)),
             dma((2, 4)), dma((2, 4)), dma((2,)), dma((2,)), dma((2, 8)), dma((2, 8)),
             dma((8,)), dma((8,)), dma((4,)),
         ],

time: 133 us -> 123 us (0.925)
  Pallas kernels: 125 us -> 114 us
    pallas_call x1, Pallas kernels: 125 us -> 114 us  [layer(): pl.pallas_call(kernel, out_shape=[jax.ShapeDtypeStruct(act, BF), jax.Shap...]
where the time goes in v3:
time: 123 us; the launch traced here: 122 us
  Pallas kernels  114 us (93%)
  local copies, waits for them, and re-layouts  5.76 us (5%)
  matrix products  1.32 us (1%)
    pallas_call x1, Pallas kernels, layer(): pl.pallas_call(kernel, out_shape=[jax.ShapeDtypeStruct(act, BF), jax.Shap...  114 us
    unnamed x15, local copies, waits for them, and re-layouts  5.12 us

profile of v3, /device:TPU:1, one launch (start us, length us, event | category | flops | bytes accessed | tf_op | source)
XLA Modules:
  0.0 122.4 jit_solution(2390666822524720867)
XLA Ops:
  0.6 0.0 copy-start
  0.6 0.0 copy-start.2
  0.7 0.0 copy-start.5
  0.7 0.7 copy-done.2
  1.4 0.0 copy-done.5
  1.4 0.1 fusion.2
  1.5 0.1 reshape.51
  1.6 0.1 copy.16
  1.6 0.1 reshape.52
  1.7 0.0 copy-start.4
  1.8 0.6 copy-done.4
  2.4 0.1 add_bitcast_fusion
  2.5 0.0 copy-start.3
  2.5 0.6 copy-done.3
  3.1 1.3 %fusion.hid = bf16[128,1024]{1,0:T(8,128)(2,1)S(1)} fusion(bf16[173,1024]{1,0:T(8,128)(2,1)} %param.10, bf16[1,128,1024]{2,1,0:T(8,128)(2,1)} %param.8, s32[128]{0:T(128)S(1)} %bitcast.24), kind=kOutput, calls=%fused_computation.1 | convolution fusion | flops 45766272 | bytes 879104 | tf_op jit(solution)/shard_map/dot_general | solution.py:676
  4.5 0.0 copy-done
  4.5 0.2 bitcast_bitcast_fusion
  4.7 0.0 copy-start.1
  4.7 0.2 reshape.50.wt
  4.9 0.7 copy-done.1
  5.6 114.4 %shard_map.103 = (bf16[128,1024]{1,0:T(8,128)(2,1)S(1)}, bf16[128,1024]{1,0:T(8,128)(2,1)S(1)}, f32[64,4,1024]{2,1,0:T(4,128)S(1)}) custom-call(bf16[128,1024]{1,0:T(8,128)(2,1)S(1)} %fusion.hid, bf16[128,1024]{1,0:T(8,128)(2,1)S(1)} %bitcast.22, bf16[8,64,512]{2,1,0:T(8,128)(2,1)S(1)} %reshape.50.wt, s32[8,128]{1,0:T(8,128)S(1)} %concatenate.7.tab), custom_call_target="tpu_custom_call" | custom-call | tf_op jit(solution)/shard_map/pallas_call | solution.py:602
  120.0 0.7 copy.22
  120.7 0.7 copy.23
  121.4 1.0 copy.24
  (4 shorter events, 0.0 us)
Async XLA Ops:
  0.6 3.8 %copy-start = (bf16[64,4,1024]{2,1,0:T(4,128)(2,1)S(1)}, bf16[64,4,1024]{2,1,0:T(4,128)(2,1)}, u32[]{:S(2)}) copy-start(bf16[64,4,1024]{2,1,0:T(4,128)(2,1)} %param.11) | copy-start | bytes 1572868
  0.6 0.7 copy-start.2
  0.7 0.7 copy-start.5
  1.7 0.7 copy-start.4
  2.5 0.7 copy-start.3
  4.7 1.0 copy-start.1

commit v4 on v3

--- a/solution.py
+++ b/solution.py
@@ -50,13 +50,14 @@
 
 
 def kernel(
-    hid, cot, wt, tab,
+    feat, labels, table, order, neigh, counts, cot, wt,
     layer_out, features_grad, proj_grad,
-    hid8, cot8, hid_t, wg, wo, w_t, tab8, tabs, stage_qk, stage_v, stage_g, land_qk, land_v, land_g,
-    v_full, probs, lows, tiles, back_a, back_q, back_kv, home_a, home_q, home_kv, mix,
-    part, total, sib, far, terms, from_y, to_z, from_z, from_zl, full, wob,
+    hid, tab, hid8, cot8, hid_t, wg, wo, w_t, tab8, raw, slots_of, users_of, stage_qk, stage_v, stage_g, land_qk, land_v, land_g,
+    v_full, probs, lows, tiles, back_a, back_q, back_k, back_v, home_a, home_q, home_k, home_v, mix,
+    part, total, sib, far, terms_a, terms_k, terms_v, from_y_a, from_y_k, from_y_v,
+    to_z_a, to_z_k, to_z_v, from_z_a, from_z_k, from_z_v, full_a, full_k, full_v, wob,
     hid_s, hid_r, hid_h, cot_s, cot_r, cot_h, tab_s, tab_r, w_s, w_r, v_s, v_r, o_s, o_r, sc_s, sc_r,
-    m_s, m_r, sib_s, sib_r, far_s, far_r, y_s, y_r, z_s, z_r, zl_s, zl_r, g_s, g_r, q_s, q_r, loc,
+    m_s, m_r, sib_s, sib_r, far_s, far_r, y_s, y_r, z_s, z_r, g_s, g_r, q_s, q_r, loc,
 ):
     dp, r = lax.axis_index("dp"), lax.axis_index("seq")
     zl, p = dp // TEAM, dp % TEAM
@@ -65,7 +66,7 @@
     base = zl * TEAM
     me = c * XS + x
     sibling = (base + x * 2 + 1 - c, r)
-    partner = (lax.rem(dp + TEAM, 2 * TEAM), r)
+    across = lax.rem(dp + TEAM, 2 * TEAM)
 
     def turn(k):
         return lax.rem(x + k, XS)
@@ -89,39 +90,52 @@
         return lax.rem(q, 2) * XS + q // 2
 
     barrier = pltpu.get_barrier_semaphore()
-    greeted = [(team_peer(k), r) for k in range(1, TEAM)]
-    greeted += [(dp, lax.rem(r + k, SEQ)) for k in range(1, SEQ)] + [partner]
+    greeted = [(lax.rem(dp + k, 2 * TEAM), r) for k in range(1, 2 * TEAM)]
+    greeted += [(dp, lax.rem(r + k, SEQ)) for k in range(1, SEQ)]
+    greeted += [(across, at_z(k)) for k in (1, 2, 3)]
     for where in greeted:
         pl.semaphore_signal(barrier, inc=1, device_id=where, device_id_type=MESH)
+    chosen = lax.broadcasted_iota(jnp.int32, (table.shape[0], ROWS), 0) == labels[...]
+    embedded = dot(chosen.astype(F32).astype(BF), table[...], TN)
+    hid[...] = (feat[...].astype(F32) + embedded).astype(BF)
+    tab[...] = jnp.zeros_like(tab)
+    tab[0:1, 0:SEQ] = order[...]
+    tab[1:2, 0:SEQ] = counts[...]
+    tab[2:6, 0:SEQ] = neigh[...]
     pl.semaphore_wait(barrier, len(greeted))
     sends = []
 
-    sources = (stage_qk, stage_v, stage_g, back_a, back_q, back_kv)
-    targets = (land_qk, land_v, land_g, home_a, home_q, home_kv)
+    sources = (stage_qk, stage_v, stage_g, back_a, back_q, back_k, back_v)
+    targets = (land_qk, land_v, land_g, home_a, home_q, home_k, home_v)
 
     def message(kind, t):
         return remote(
             sources[kind].at[t], targets[kind].at[r], m_s.at[kind, t], m_r.at[kind, r], (dp, t)
         )
 
-    def give(kind, t):
-        @pl.when(t != r)
-        def _():
-            message(kind, t).start()
-
-        @pl.when(t == r)
-        def _():
-            targets[kind][r] = sources[kind][t]
-
-    def got(kind, t):
-        @pl.when(t != r)
-        def _():
-            arrival(targets[kind].at[t], m_r.at[kind, t], (dp, t))
+    def after(k):
+        return lax.rem(r + k, SEQ)
+
+    def before(k):
+        return lax.rem(r + SEQ - k, SEQ)
+
+    def keep(kind):
+        targets[kind][r] = sources[kind][r]
+
+    def arrived(kind, t):
+        arrival(targets[kind].at[t], m_r.at[kind, t], (dp, t))
+
+    def give_all(kind):
+        def one(k, carry):
+            message(kind, after(k)).start()
+            return carry
+
+        lax.fori_loop(1, SEQ, one, 0)
+        keep(kind)
 
     def got_all(kind):
         def one(k, carry):
-            t = lax.rem(r + k, SEQ)
-            arrival(targets[kind].at[t], m_r.at[kind, t], (dp, t))
+            arrived(kind, before(k))
             return carry
 
         lax.fori_loop(1, SEQ, one, 0)
@@ -170,10 +184,12 @@
     mine_qk, mine_v = wt.at[p, :, 0:256], wt.at[p, :, 256:384]
     for k in NEAR:
         sends.append(push(mine_qk, qk_part(r), w_s.at[k], w_r.at[r], (dp, at_z(k))))
-        sends.append(push(mine_v, v_part(r), v_s.at[k], v_r.at[r], (dp, at_y(k))))
     for k in NEAR:
         sends.append(push(mine_qk, qk_part(r), w_s.at[3 + k], w_r.at[r], (dp, at_y(k))))
-        sends.append(push(mine_v, v_part(r), v_s.at[3 + k], v_r.at[r], (dp, at_z(k))))
+    for k in NEAR:
+        sends.append(push(mine_v, v_part(r), v_s.at[k], v_r.at[r], (dp, at_z(k))))
+    for k in NEAR:
+        sends.append(push(mine_v, v_part(r), v_s.at[3 + k], v_r.at[r], (dp, at_y(k))))
 
     spread = r // 2 == p
 
@@ -201,15 +217,16 @@
             sends.append(
                 push(qk_part(s), qk_part(s), w_s.at[7 + n * 3 + m], w_r.at[s], (dp, at_y(m)))
             )
-        s = at_y(k)
+
+    forward_x(hid8, hid_s, hid_r, hid_h)
+    spread_x(cot8, cot, cot_s, cot_r)
+    for n, k in enumerate(NEAR):
+        s = at_z(k)
         arrival(v_part(s), v_r.at[s], (dp, s))
         for m in NEAR:
             sends.append(
-                push(v_part(s), v_part(s), v_s.at[7 + n * 3 + m], v_r.at[s], (dp, at_z(m)))
+                push(v_part(s), v_part(s), v_s.at[7 + n * 3 + m], v_r.at[s], (dp, at_y(m)))
             )
-
-    forward_x(hid8, hid_s, hid_r, hid_h)
-    spread_x(cot8, cot, cot_s, cot_r)
 
     piece = out_part(r)
 
@@ -246,15 +263,13 @@
         block = array[pl.ds(pl.multiple_of(core * XS, XS), XS)]
         return block.reshape(HALF, array.shape[2])
 
-    def packed(stage, kind, core, result):
+    def packed(stage, core, result):
         for n in range(XS):
             top = result[n * ROWS : n * ROWS + 64]
             bottom = result[n * ROWS + 64 : n * ROWS + ROWS]
             i = core * XS + n
             stage[2 * i] = merge(top, bottom)
             stage[2 * i + 1] = merge_high(top, bottom)
-            give(kind, 2 * i)
-            give(kind, 2 * i + 1)
 
     from_all_y(qk_part, w_r)
     own_w.wait()
@@ -269,19 +284,13 @@
             i = core * XS + n
             stage_qk[2 * i] = merge(q, k)
             stage_qk[2 * i + 1] = merge_high(q, k)
-            give(0, 2 * i)
-            give(0, 2 * i + 1)
+    give_all(0)
 
     forward_x(cot8, cot_s, cot_r, cot_h)
-    for m in NEAR:
-        for k in range(1, 4):
-            s = lax.rem(zh + k, 4) * YS + lax.rem(y + m, YS)
-            arrival(v_part(s), v_r.at[s], (dp, s))
-    for k in NEAR:
-        s = at_z(k)
-        arrival(v_part(s), v_r.at[s], (dp, s))
+    from_all_y(v_part, v_r)
     for core in (c, 1 - c):
-        packed(stage_v, 1, core, dot(group_rows(hid8, core), wg[:, 256:384]).astype(BF))
+        packed(stage_v, core, dot(group_rows(hid8, core), wg[:, 256:384]).astype(BF))
+    give_all(1)
     from_all_y(out_part, o_r)
     for j in range(TEAM):
         block = wg[128 * j : 128 * j + 128, 384:512]
@@ -292,7 +301,9 @@
     for core in (c, 1 - c):
         if core is not c:
             other_core(cot8, cot_r)
-        packed(stage_g, 2, core, dot(group_rows(cot8, core), wo[...]).astype(BF))
+        packed(stage_g, core, dot(group_rows(cot8, core), wo[...]).astype(BF))
+
+    give_all(2)
 
     for n in range(3):
         w_t[128 * n : 128 * n + 128, :] = wg[:, 128 * n : 128 * n + 128].T
@@ -304,9 +315,24 @@
         q = slot_of(i)
         arrival(tab8.at[q], tab_r.at[q], (base + i, r))
     tab8[me] = tab[...]
-    to_scalars = pltpu.make_async_copy(tab8.at[r // 2], tabs, loc.at[3])
+    to_scalars = pltpu.make_async_copy(tab8.at[r // 2], raw, loc.at[3])
     to_scalars.start()
     to_scalars.wait()
+
+    def list_blocks(s, carry):
+        for b in range(SEQ):
+            users_of[b, s] = 64
+        for j in range(4):
+            name = raw[2 + j, s]
+            found = 0
+            for b in range(SEQ):
+                hit = raw[0, b] == name
+                found = jnp.where(hit, b, found)
+                users_of[b, s] = jnp.where(hit, 4 * s + j, users_of[b, s])
+            slots_of[s, j] = found
+        return carry
+
+    lax.fori_loop(0, SEQ, list_blocks, 0)
 
     lo = low_lanes((128, 128))
     zero = jnp.zeros((128, 128), BF)
@@ -314,9 +340,9 @@
 
     def probabilities(s):
         qz = jnp.where(lo, zero, pltpu.roll(land_qk[s], 64, 1)) * jnp.asarray(0.125, BF)
-        count = tabs[2, 64 + s]
+        count = raw[1, s]
         scores = [
-            jnp.where(j < count, dot(land_qk[tabs[2, 4 * s + j]], qz, NT), -1e30) for j in range(4)
+            jnp.where(j < count, dot(land_qk[slots_of[s, j]], qz, NT), -1e30) for j in range(4)
         ]
         top = jnp.max(
             jnp.maximum(jnp.maximum(scores[0], scores[1]), jnp.maximum(scores[2], scores[3])),
@@ -345,16 +371,26 @@
     def blocks_of(g):
         return [lax.rem(r + 1 + 4 * g + n, SEQ) for n in range(4)]
 
+    def hand_over(kind, g):
+        for n, s in enumerate(blocks_of(g)):
+            if n < 3:
+                message(kind, s).start()
+            else:
+
+                @pl.when(s != r)
+                def _():
+                    message(kind, s).start()
+
     def attention(g, carry):
         for s in blocks_of(g):
-            values = [v_full[tabs[2, 4 * s + j]] for j in range(4)]
+            values = [v_full[slots_of[s, j]] for j in range(4)]
             attn = dot(jnp.concatenate(values, axis=0), lows[s], TN).T.astype(BF)
             back_a[s] = merge(attn[0:64], attn[64:128])
-        for s in blocks_of(g):
-            give(3, s)
+        hand_over(3, g)
         return carry
 
     lax.fori_loop(0, 4, attention, 0)
+    keep(3)
     got_all(2)
 
     def gradients(s):
@@ -363,7 +399,7 @@
         gz = jnp.where(lo, jnp.concatenate([grad, turned], axis=0), zero)
         gv = jnp.where(lo, zero, jnp.concatenate([turned, grad], axis=0))
         rhs = jnp.concatenate([jnp.where(lo, qk, zero), gv], axis=0)
-        slots = [tabs[2, 4 * s + j] for j in range(4)]
+        slots = [slots_of[s, j] for j in range(4)]
         keys = [land_qk[b] for b in slots]
         grad_p = [dot(v_full[b], gz, NT) for b in slots]
         prob = [probs[s, j] for j in range(4)]
@@ -381,23 +417,26 @@
     def backward(g, carry):
         for s in blocks_of(g):
             gradients(s)
-        for s in blocks_of(g):
-            give(4, s)
+        hand_over(4, g)
         return carry
 
     lax.fori_loop(0, 4, backward, 0)
+    keep(4)
     tiles[64] = jnp.zeros((128, 128), F32)
 
     def collect(n, carry):
         b = lax.rem(r + 1 + n, SEQ)
-        total = tiles[tabs[b // 8, (b % 8) * 16]]
+        total = tiles[users_of[b, 0]]
         for s in range(1, SEQ):
-            total += tiles[tabs[b // 8, (b % 8) * 16 + s]]
-        back_kv[b] = total.astype(BF)
-        give(5, b)
+            total += tiles[users_of[b, s]]
+        low = total.astype(BF)
+        back_k[b] = merge(low[0:64], low[64:128])
+        back_v[b] = merge_high(low[0:64], low[64:128])
         return carry
 
     lax.fori_loop(0, SEQ, collect, 0)
+
+    give_all(5)
 
     def half_rows(core):
         return pl.ds(pl.multiple_of(core * HALF, HALF), HALF)
@@ -405,17 +444,11 @@
     def take(core, kind):
         for n in range(XS):
             i = core * XS + n
-            got(kind, 2 * i)
-            got(kind, 2 * i + 1)
             a, b = targets[kind][2 * i], targets[kind][2 * i + 1]
             start = pl.multiple_of(i * ROWS, ROWS)
-            if kind == 5:
-                mix[pl.ds(start, ROWS), 256:384] = merge(a, b)
-                mix[pl.ds(start, ROWS), 384:512] = merge_high(a, b)
-            else:
-                cols = pl.ds(128 * (kind - 3), 128)
-                mix[pl.ds(start, 64), cols] = merge(a, b)
-                mix[pl.ds(start + 64, 64), cols] = merge_high(a, b)
+            cols = pl.ds(128 * (kind - 3), 128)
+            mix[pl.ds(start, 64), cols] = merge(a, b)
+            mix[pl.ds(start + 64, 64), cols] = merge_high(a, b)
 
     def product(core, n):
         if n == 0:
@@ -450,93 +483,113 @@
             result += far[n, turn(k)].astype(F32)
         return result.astype(BF)
 
-    def terms_out(n):
-        if n == 0:
+    terms = (terms_a, terms_k, terms_v)
+    from_y = (from_y_a, from_y_k, from_y_v)
+    to_z = (to_z_a, to_z_k, to_z_v)
+    from_z = (from_z_a, from_z_k, from_z_v)
+    full = (full_a, full_k, full_v)
+
+    def terms_out(g):
+        if g == 0:
             cots = cot8[...].reshape(TEAM * ROWS, WIDTH)
             out_term = dot(mix[:, 0:128], cots, TN).astype(BF)
             for j in range(TEAM):
                 block = out_term[:, 128 * j : 128 * j + 128]
-                terms[0, 2 * j, :, 128:256] = block[0:64]
-                terms[0, 2 * j + 1, :, 128:256] = block[64:128]
-            in_term = dot(hid_t[...], mix[:, 128:256]).astype(BF)
-            for s in range(SEQ):
-                terms[0, s, :, 0:128] = in_term[64 * s : 64 * s + 64]
+                terms_a[2 * j, :, 128:256] = block[0:64]
+                terms_a[2 * j + 1, :, 128:256] = block[64:128]
+        first = 128 * (g + 1)
         for h in range(4):
-            if n == 1:
-                in_term = dot(hid_t[256 * h : 256 * h + 256], mix[:, 256:512]).astype(BF)
-                for m in range(YS):
-                    terms[1, 4 * h + m] = in_term[64 * m : 64 * m + 64]
+            rows = hid_t[256 * h : 256 * h + 256]
+            in_term = dot(rows, mix[:, first : first + 128]).astype(BF)
+            for m in range(YS):
+                terms[g][4 * h + m, :, 0:128] = in_term[64 * m : 64 * m + 64]
             for k in NEAR:
                 sends.append(
                     push(
-                        terms.at[n, 4 * h + lax.rem(y + k, YS)], from_y.at[n, y, h],
-                        y_s.at[n, k, h], y_r.at[n, y, h], (dp, at_y(k)),
+                        terms[g].at[4 * h + lax.rem(y + k, YS)], from_y[g].at[y, h],
+                        y_s.at[g, k, h], y_r.at[g, y, h], (dp, at_y(k)),
                     )
                 )
 
-    def along_z(n):
-        for k in (1, 2, 3, 0):
+    def half_of(side):
+        return pl.ds(pl.multiple_of(side * 32, 32), 32)
+
+    def along_z(g):
+        for k in (2, 1, 3, 0):
             h = lax.rem(zh + k, 4)
-            total = terms[n, 4 * h + y].astype(F32)
+            result = terms[g][4 * h + y].astype(F32)
             for m in NEAR:
                 t = lax.rem(y + m, YS)
-                arrival(from_y.at[n, t, h], y_r.at[n, t, h], (dp, at_y(m)))
-                total += from_y[n, t, h].astype(F32)
-            to_z[n, h] = total.astype(BF)
-            if k:
-                sends.append(
-                    push(
-                        to_z.at[n, h], from_z.at[n, zh], z_s.at[n, h], z_r.at[n, zh],
-                        (dp, h * YS + y),
+                arrival(from_y[g].at[t, h], y_r.at[g, t, h], (dp, at_y(m)))
+                result += from_y[g][t, h].astype(F32)
+            to_z[g][h] = result.astype(BF)
+            for other in (0, 1):
+                if k or other:
+                    side = lax.rem(zl + other, 2)
+                    where = across if other else dp
+                    sends.append(
+                        push(
+                            to_z[g].at[h, half_of(side)], from_z[g].at[zl, zh],
+                            z_s.at[g, other, h], z_r.at[g, zl, zh], (where, h * YS + y),
+                        )
                     )
-                )
-
-    def across(n):
-        total = to_z[n, zh].astype(F32)
-        for k in NEAR:
+
+    def to_team(g):
+        result = to_z[g][zh, half_of(zl)].astype(F32)
+        for k in (1, 3, 2, 0):
             h = lax.rem(zh + k, 4)
-            arrival(from_z.at[n, h], z_r.at[n, h], (dp, at_z(k)))
-            total += from_z[n, h].astype(F32)
-        from_z[n, zh] = total.astype(BF)
-        sends.append(push(from_z.at[n, zh], from_zl.at[n], zl_s.at[n], zl_r.at[n], partner))
-
-    def to_team(n):
-        arrival(from_zl.at[n], zl_r.at[n], partner)
-        full[n, me] = (from_z[n, zh].astype(F32) + from_zl[n].astype(F32)).astype(BF)
-        for k in range(1, TEAM):
-            sends.append(
-                push(
-                    full.at[n, me], full.at[n, me], g_s.at[n, k], g_r.at[n, me], (team_peer(k), r)
-                )
-            )
-
-    def from_team(n):
-        for k in range(1, TEAM):
-            i = lax.rem(p + k, TEAM)
-            q = slot_of(i)
-            arrival(full.at[n, q], g_r.at[n, q], (base + i, r))
+            for other in (0, 1):
+                if k or other:
+                    side = lax.rem(zl + other, 2)
+                    arrival(from_z[g].at[side, h], z_r.at[g, side, h], (dp, at_z(k)))
+                    result += from_z[g][side, h].astype(F32)
+        piece = full[g].at[me, half_of(zl)]
+        piece[...] = result.astype(BF)
+        for k in range(1, 2 * TEAM):
+            where = lax.rem(dp + k, 2 * TEAM)
+            sends.append(push(piece, piece, g_s.at[g, k], g_r.at[g, zl, me], (where, r)))
+
+    def from_team(g):
+        for k in range(1, 2 * TEAM):
+            other = lax.rem(dp + k, 2 * TEAM)
+            side, q = other // TEAM, slot_of(other % TEAM)
+            arrival(full[g].at[q, half_of(side)], g_r.at[g, side, q], (other, r))
 
     def out_piece(i):
         t = 2 * i + r % 2
-        src = full.at[0, (i % 2) * XS + i // 2, :, 128:256]
+        src = full_a.at[(i % 2) * XS + i // 2, :, 128:256]
         return t, remote(src, wob.at[r // 2], q_s.at[i], q_r.at[r // 2], (dp, t))
 
-    take(1 - c, 3)
+    def write(g):
+        for i in range(TEAM):
+            q = (i % 2) * XS + i // 2
+            proj_grad[:, g, 128 * i : 128 * i + 128] = full[g][q, :, 0:128].astype(F32)
+
+    def take_all(kind):
+        take(0, kind)
+        take(1, kind)
+
+    got_all(3)
+    take_all(3)
     share(0)
-    take(c, 3)
     pass_on(0)
-    take(1 - c, 4)
-    take(c, 4)
+    give_all(6)
+    got_all(4)
+    take_all(4)
     terms_out(0)
-    take(1 - c, 5)
-    take(c, 5)
+    got_all(5)
+    take_all(5)
     terms_out(1)
+    along_z(0)
+    got_all(6)
+    take_all(6)
+    terms_out(2)
     share(1)
-    along_z(0)
-    pass_on(1)
-    across(0)
     to_team(0)
     along_z(1)
+    pass_on(1)
+    to_team(1)
+    along_z(2)
     layer_out[...] = result_of(0, hid8[me])
     from_team(0)
     for i in range(TEAM):
@@ -548,13 +601,12 @@
 
         @pl.when(t == r)
         def _():
-            wob[r // 2] = full[0, (i % 2) * XS + i // 2, :, 128:256]
-
-    across(1)
-    for i in range(TEAM):
-        q = (i % 2) * XS + i // 2
-        proj_grad[:, 0, 128 * i : 128 * i + 128] = full[0, q, :, 0:128].astype(F32)
-    to_team(1)
+            wob[r // 2] = full_a[(i % 2) * XS + i // 2, :, 128:256]
+
+    write(0)
+    to_team(2)
+    from_team(1)
+    write(1)
     for j in range(TEAM):
         t, copy = out_piece(j)
 
@@ -565,11 +617,8 @@
 
         proj_grad[:, 3, 128 * j : 128 * j + 128] = wob[j].astype(F32)
     features_grad[...] = result_of(1, cot8[me])
-    from_team(1)
-    for i in range(TEAM):
-        q = (i % 2) * XS + i // 2
-        proj_grad[:, 1, 128 * i : 128 * i + 128] = full[1, q, :, 0:128].astype(F32)
-        proj_grad[:, 2, 128 * i : 128 * i + 128] = full[1, q, :, 128:256].astype(F32)
+    from_team(2)
+    write(2)
 
     for copy in sends:
         copy.wait_send()
@@ -587,18 +636,19 @@
 
     def sent(k, carry):
         t = lax.rem(r + k, SEQ)
-        for kind in range(6):
+        for kind in range(7):
             message(kind, t).wait_send()
         return carry
 
     lax.fori_loop(1, SEQ, sent, 0)
 
 
-def layer(hid, cot, wt, tab):
+def layer(feat, labels, table, order, neigh, counts, cot, wt):
     vmem = pl.BlockSpec(memory_space=pltpu.VMEM)
     dma = pltpu.SemaphoreType.DMA
     tile, small = (128, 128), (64, 128)
     act = (ROWS, WIDTH)
+    widths = (256, 128, 128)
     return pl.pallas_call(
         kernel,
         out_shape=[
@@ -606,9 +656,11 @@
             jax.ShapeDtypeStruct(act, BF),
             jax.ShapeDtypeStruct((SHARD, 4, WIDTH), F32),
         ],
-        in_specs=[vmem] * 4,
+        in_specs=[vmem] * 8,
         out_specs=[vmem] * 3,
         scratch_shapes=[
+            pltpu.VMEM(act, BF),
+            pltpu.VMEM((8, 128), jnp.int32),
             pltpu.VMEM((TEAM, *act), BF),
             pltpu.VMEM((TEAM, *act), BF),
             pltpu.VMEM((WIDTH, TEAM * ROWS), BF),
@@ -617,6 +669,8 @@
             pltpu.VMEM((512, WIDTH), BF),
             pltpu.VMEM((TEAM, 8, 128), jnp.int32),
             pltpu.SMEM((8, 128), jnp.int32),
+            pltpu.SMEM((SEQ, 4), jnp.int32),
+            pltpu.SMEM((SEQ, SEQ), jnp.int32),
             pltpu.VMEM((SEQ, *tile), BF),
             pltpu.VMEM((SEQ, *small), BF),
             pltpu.VMEM((SEQ, *small), BF),
@@ -627,57 +681,37 @@
             pltpu.VMEM((SEQ, 4, *tile), F32),
             pltpu.VMEM((SEQ, 512, 128), BF),
             pltpu.VMEM((SEQ * 4 + 1, *tile), F32),
-            pltpu.VMEM((SEQ, *small), BF),
-            pltpu.VMEM((SEQ, *small), BF),
-            pltpu.VMEM((SEQ, *tile), BF),
-            pltpu.VMEM((SEQ, *small), BF),
-            pltpu.VMEM((SEQ, *small), BF),
-            pltpu.VMEM((SEQ, *tile), BF),
+            *[pltpu.VMEM((SEQ, *small), BF)] * 8,
             pltpu.VMEM((TEAM * ROWS, 512), BF),
             pltpu.VMEM((2, 2 * XS, *act), BF),
             pltpu.VMEM((XS, *act), F32),
             pltpu.VMEM((2, XS, *act), BF),
             pltpu.VMEM((2, XS, *act), BF),
-            pltpu.VMEM((2, SEQ, SHARD, 256), BF),
-            pltpu.VMEM((2, YS, 4, SHARD, 256), BF),
-            pltpu.VMEM((2, 4, SHARD, 256), BF),
-            pltpu.VMEM((2, 4, SHARD, 256), BF),
-            pltpu.VMEM((2, SHARD, 256), BF),
-            pltpu.VMEM((2, TEAM, SHARD, 256), BF),
+            *[pltpu.VMEM((SEQ, SHARD, w), BF) for w in widths],
+            *[pltpu.VMEM((YS, 4, SHARD, w), BF) for w in widths],
+            *[pltpu.VMEM((4, SHARD, w), BF) for w in widths],
+            *[pltpu.VMEM((2, 4, SHARD // 2, w), BF) for w in widths],
+            *[pltpu.VMEM((TEAM, SHARD, w), BF) for w in widths],
             pltpu.VMEM((TEAM, SHARD, 128), BF),
             dma((8,)), dma((8,)), dma((2,)), dma((8,)), dma((8,)), dma((2,)), dma((8,)), dma((8,)),
             dma((17,)), dma((16,)), dma((17,)), dma((16,)), dma((17,)), dma((16,)), dma((8,)), dma(()),
-            dma((6, 16)), dma((6, 16)),
-            dma((2, 4)), dma((2, 4)), dma((2, 4)), dma((2, 4)), dma((2, 4, 4)), dma((2, 4, 4)),
-            dma((2, 4)), dma((2, 4)), dma((2,)), dma((2,)), dma((2, 8)), dma((2, 8)),
-            dma((8,)), dma((8,)), dma((4,)),
+            dma((7, 16)), dma((7, 16)),
+            dma((2, 4)), dma((2, 4)), dma((2, 4)), dma((2, 4)), dma((3, 4, 4)), dma((3, 4, 4)),
+            dma((3, 2, 4)), dma((3, 2, 4)), dma((3, 16)), dma((3, 2, 8)), dma((8,)), dma((8,)), dma((4,)),
         ],
         compiler_params=pltpu.CompilerParams(
             collective_id=1, has_side_effects=True, vmem_limit_bytes=VMEM_BYTES
         ),
-    )(hid, cot, wt, tab)
-
-
-def tables(order, neigh, count):
-    spots = lax.iota(jnp.int32, SEQ)
-    listing = 4 * spots[:, None] + lax.iota(jnp.int32, 4)[None, :]
-    named = neigh[None] == order[:, None, None]
-    users = jnp.min(jnp.where(named, listing[None], 64), axis=2)
-    slots = jnp.sum(jnp.where(named, spots[:, None, None], 0), axis=0)
-    flat = jnp.concatenate([users.reshape(-1), slots.reshape(-1), count, jnp.zeros((48,), jnp.int32)])
-    return jnp.concatenate([flat.reshape(3, 128), jnp.zeros((5, 128), jnp.int32)])
+    )(feat, labels, table, order, neigh, counts, cot, wt)
 
 
 def per_device(
     features, labels, label_table, proj_weight, block_order, neighbours, counts, cotangent
 ):
-    onehot = (labels[0][:, None] == lax.iota(jnp.int32, label_table.shape[0])[None, :]).astype(BF)
-    hidden = (
-        features[0].astype(F32) + jnp.dot(onehot, label_table, preferred_element_type=F32)
-    ).astype(BF)
     wt = proj_weight.reshape(SHARD, 4, TEAM, 128).transpose(2, 0, 1, 3).reshape(TEAM, SHARD, 512)
-    tab = tables(block_order[0], neighbours[0], counts[0])
-    layer_out, features_grad, proj_grad = layer(hidden, cotangent[0], wt, tab)
+    layer_out, features_grad, proj_grad = layer(
+        features[0], labels, label_table, block_order, neighbours[0].T, counts, cotangent[0], wt
+    )
     return (layer_out[None], features_grad[None], proj_grad)
 
 

time: 123 us -> 119 us (0.967)
  matrix products: 1.32 us -> 0 us
    dot_general x1 -> x0, matrix products: 1.32 us -> none  [per_device(): jnp.dot(onehot, label_table, preferred_element_type=F32)]
    unnamed x15 -> x19, local copies, waits for them, and re-layouts: 5.12 us -> 4.31 us
where the time goes in v4:
time: 119 us
  Pallas kernels  113 us (95%)
  local copies, waits for them, and re-layouts  4.69 us (4%)
    pallas_call x1, Pallas kernels, layer(): pl.pallas_call(kernel, out_shape=[jax.ShapeDtypeStruct(act, BF), jax.Shap...  113 us
    unnamed x19, local copies, waits for them, and re-layouts  4.31 us

profile of v4, /device:TPU:1, one launch (start us, length us, event | category | flops | bytes accessed | tf_op | source)
XLA Modules:
  0.0 118.7 jit_solution(750320943927082206)
XLA Ops:
  0.6 0.0 copy-start
  0.6 1.0 copy-done
  1.7 0.2 bitcast_bitcast_fusion
  1.9 0.0 copy-start.1
  1.9 0.0 copy-start.2
  1.9 0.0 copy-start.3
  1.9 0.0 copy-start.4
  1.9 0.0 copy-start.5
  1.9 0.0 copy-start.6
  1.9 0.0 copy-start.7
  1.9 0.2 reshape.13.wt
  2.2 0.7 copy-done.1
  2.9 0.1 copy-done.2
  2.9 0.1 copy-done.3
  3.0 0.0 copy-done.4
  3.0 0.0 copy-done.5
  3.0 0.0 copy-done.6
  3.0 0.0 copy-done.7
  3.0 113.3 %shard_map.103 = (bf16[128,1024]{1,0:T(8,128)(2,1)S(1)}, bf16[128,1024]{1,0:T(8,128)(2,1)S(1)}, f32[64,4,1024]{2,1,0:T(4,128)S(1)}) custom-call(bf16[128,1024]{1,0:T(8,128)(2,1)S(1)} %bitcast.16, s32[1,128]{1,0:T(1,128)S(1)} %copy-done.5, bf16[173,1024]{1,0:T(8,128)(2,1)S(1)} %copy-done.1, s32[1,16]{1,0:T(1,128)S(1)} %copy-done.6, s32[4,16]{1,0:T(4,128)S(1)} %bitcast.18, ...), custom_call_target="tpu_custom_call" | custom-call | tf_op jit(solution)/shard_map/pallas_call | solution.py:652
  116.3 0.7 copy.17
  117.0 0.7 copy.18
  117.7 1.0 copy.19
Async XLA Ops:
  0.6 1.0 copy-start
  1.9 1.0 copy-start.1
  1.9 1.1 copy-start.2
  1.9 1.1 copy-start.3
  1.9 1.1 copy-start.4
  1.9 1.1 copy-start.5
  1.9 1.1 copy-start.6
  1.9 1.1 copy-start.7

commit v5 on v4

--- a/solution.py
+++ b/solution.py
@@ -54,8 +54,8 @@
     layer_out, features_grad, proj_grad,
     hid, tab, hid8, cot8, hid_t, wg, wo, w_t, tab8, raw, slots_of, users_of, stage_qk, stage_v, stage_g, land_qk, land_v, land_g,
     v_full, probs, lows, tiles, back_a, back_q, back_k, back_v, home_a, home_q, home_k, home_v, mix,
-    part, total, sib, far, terms_a, terms_k, terms_v, from_y_a, from_y_k, from_y_v,
-    to_z_a, to_z_k, to_z_v, from_z_a, from_z_k, from_z_v, full_a, full_k, full_v, wob,
+    part, total, sib, far, terms_o, terms_q, terms_kv, from_y_o, from_y_q, from_y_kv,
+    to_z_o, to_z_q, to_z_kv, from_z_o, from_z_q, from_z_kv, full_o, full_q, full_kv, wob,
     hid_s, hid_r, hid_h, cot_s, cot_r, cot_h, tab_s, tab_r, w_s, w_r, v_s, v_r, o_s, o_r, sc_s, sc_r,
     m_s, m_r, sib_s, sib_r, far_s, far_r, y_s, y_r, z_s, z_r, g_s, g_r, q_s, q_r, loc,
 ):
@@ -432,11 +432,17 @@
         low = total.astype(BF)
         back_k[b] = merge(low[0:64], low[64:128])
         back_v[b] = merge_high(low[0:64], low[64:128])
+
+        @pl.when(n < SEQ - 1)
+        def _():
+            message(5, b).start()
+            message(6, b).start()
+
         return carry
 
     lax.fori_loop(0, SEQ, collect, 0)
-
-    give_all(5)
+    keep(5)
+    keep(6)
 
     def half_rows(core):
         return pl.ds(pl.multiple_of(core * HALF, HALF), HALF)
@@ -483,11 +489,11 @@
             result += far[n, turn(k)].astype(F32)
         return result.astype(BF)
 
-    terms = (terms_a, terms_k, terms_v)
-    from_y = (from_y_a, from_y_k, from_y_v)
-    to_z = (to_z_a, to_z_k, to_z_v)
-    from_z = (from_z_a, from_z_k, from_z_v)
-    full = (full_a, full_k, full_v)
+    terms = (terms_o, terms_q, terms_kv)
+    from_y = (from_y_o, from_y_q, from_y_kv)
+    to_z = (to_z_o, to_z_q, to_z_kv)
+    from_z = (from_z_o, from_z_q, from_z_kv)
+    full = (full_o, full_q, full_kv)
 
     def terms_out(g):
         if g == 0:
@@ -495,14 +501,14 @@
             out_term = dot(mix[:, 0:128], cots, TN).astype(BF)
             for j in range(TEAM):
                 block = out_term[:, 128 * j : 128 * j + 128]
-                terms_a[2 * j, :, 128:256] = block[0:64]
-                terms_a[2 * j + 1, :, 128:256] = block[64:128]
-        first = 128 * (g + 1)
+                terms_o[2 * j] = block[0:64]
+                terms_o[2 * j + 1] = block[64:128]
         for h in range(4):
-            rows = hid_t[256 * h : 256 * h + 256]
-            in_term = dot(rows, mix[:, first : first + 128]).astype(BF)
-            for m in range(YS):
-                terms[g][4 * h + m, :, 0:128] = in_term[64 * m : 64 * m + 64]
+            if g:
+                cols = mix[:, 128 * g : 256 * g]
+                in_term = dot(hid_t[256 * h : 256 * h + 256], cols).astype(BF)
+                for m in range(YS):
+                    terms[g][4 * h + m] = in_term[64 * m : 64 * m + 64]
             for k in NEAR:
                 sends.append(
                     push(
@@ -557,13 +563,14 @@
 
     def out_piece(i):
         t = 2 * i + r % 2
-        src = full_a.at[(i % 2) * XS + i // 2, :, 128:256]
+        src = full_o.at[(i % 2) * XS + i // 2]
         return t, remote(src, wob.at[r // 2], q_s.at[i], q_r.at[r // 2], (dp, t))
 
-    def write(g):
+    def write(n, source, first):
         for i in range(TEAM):
             q = (i % 2) * XS + i // 2
-            proj_grad[:, g, 128 * i : 128 * i + 128] = full[g][q, :, 0:128].astype(F32)
+            piece = source[q, :, first : first + 128]
+            proj_grad[:, n, 128 * i : 128 * i + 128] = piece.astype(F32)
 
     def take_all(kind):
         take(0, kind)
@@ -572,15 +579,14 @@
     got_all(3)
     take_all(3)
     share(0)
+    terms_out(0)
     pass_on(0)
-    give_all(6)
     got_all(4)
     take_all(4)
-    terms_out(0)
+    terms_out(1)
+    along_z(0)
     got_all(5)
     take_all(5)
-    terms_out(1)
-    along_z(0)
     got_all(6)
     take_all(6)
     terms_out(2)
@@ -588,25 +594,23 @@
     to_team(0)
     along_z(1)
     pass_on(1)
+    from_team(0)
+    for i in range(TEAM):
+        t, copy = out_piece(i)
+
+        @pl.when(t != r)
+        def _():
+            copy.start()
+
+        @pl.when(t == r)
+        def _():
+            wob[r // 2] = full_o[(i % 2) * XS + i // 2]
+
     to_team(1)
     along_z(2)
     layer_out[...] = result_of(0, hid8[me])
-    from_team(0)
-    for i in range(TEAM):
-        t, copy = out_piece(i)
-
-        @pl.when(t != r)
-        def _():
-            copy.start()
-
-        @pl.when(t == r)
-        def _():
-            wob[r // 2] = full_a[(i % 2) * XS + i // 2, :, 128:256]
-
-    write(0)
-    to_team(2)
     from_team(1)
-    write(1)
+    write(0, full_q, 0)
     for j in range(TEAM):
         t, copy = out_piece(j)
 
@@ -616,9 +620,11 @@
             copy.wait_send()
 
         proj_grad[:, 3, 128 * j : 128 * j + 128] = wob[j].astype(F32)
+    to_team(2)
     features_grad[...] = result_of(1, cot8[me])
     from_team(2)
-    write(2)
+    write(1, full_kv, 0)
+    write(2, full_kv, 128)
 
     for copy in sends:
         copy.wait_send()
@@ -648,7 +654,7 @@
     dma = pltpu.SemaphoreType.DMA
     tile, small = (128, 128), (64, 128)
     act = (ROWS, WIDTH)
-    widths = (256, 128, 128)
+    widths = (128, 128, 256)
     return pl.pallas_call(
         kernel,
         out_shape=[
@@ -656,7 +662,7 @@
             jax.ShapeDtypeStruct(act, BF),
             jax.ShapeDtypeStruct((SHARD, 4, WIDTH), F32),
         ],
-        in_specs=[vmem] * 8,
+        in_specs=[vmem] * 6 + [pl.BlockSpec(memory_space=pl.ANY), vmem],
         out_specs=[vmem] * 3,
         scratch_shapes=[
             pltpu.VMEM(act, BF),

time: 119 us -> 117 us (0.983)
  Pallas kernels: 113 us -> 111 us
    pallas_call x1, Pallas kernels: 113 us -> 111 us  [layer(): pl.pallas_call(kernel, out_shape=[jax.ShapeDtypeStruct(act, BF), jax.Shap...]
where the time goes in v5:
time: 117 us
  Pallas kernels  111 us (95%)
  local copies, waits for them, and re-layouts  4.69 us (4%)
    pallas_call x1, Pallas kernels, layer(): pl.pallas_call(kernel, out_shape=[jax.ShapeDtypeStruct(act, BF), jax.Shap...  111 us
    unnamed x19, local copies, waits for them, and re-layouts  4.31 us

profile of v5, /device:TPU:1, one launch (start us, length us, event | category | flops | bytes accessed | tf_op | source)
XLA Modules:
  0.0 116.5 jit_solution(1460294668911818592)
XLA Ops:
  0.6 0.0 copy-start
  0.6 1.0 copy-done
  1.7 0.2 bitcast_bitcast_fusion
  1.9 0.0 copy-start.1
  1.9 0.0 copy-start.2
  1.9 0.0 copy-start.3
  1.9 0.0 copy-start.4
  1.9 0.0 copy-start.5
  1.9 0.0 copy-start.6
  1.9 0.0 copy-start.7
  1.9 0.2 reshape.13.wt
  2.2 0.7 copy-done.1
  2.9 0.1 copy-done.2
  2.9 0.1 copy-done.3
  3.0 0.0 copy-done.4
  3.0 0.0 copy-done.5
  3.0 0.0 copy-done.6
  3.0 0.0 copy-done.7
  3.0 111.1 %shard_map.103 = (bf16[128,1024]{1,0:T(8,128)(2,1)S(1)}, bf16[128,1024]{1,0:T(8,128)(2,1)S(1)}, f32[64,4,1024]{2,1,0:T(4,128)S(1)}) custom-call(bf16[128,1024]{1,0:T(8,128)(2,1)S(1)} %bitcast.16, s32[1,128]{1,0:T(1,128)S(1)} %copy-done.5, bf16[173,1024]{1,0:T(8,128)(2,1)S(1)} %copy-done.1, s32[1,16]{1,0:T(1,128)S(1)} %copy-done.6, s32[4,16]{1,0:T(4,128)S(1)} %bitcast.18, ...), custom_call_target="tpu_custom_call" | custom-call | tf_op jit(solution)/shard_map/pallas_call | solution.py:658
  114.1 0.7 copy.17
  114.8 0.7 copy.18
  115.5 1.0 copy.19
Async XLA Ops:
  0.6 1.0 copy-start
  1.9 1.0 copy-start.1
  1.9 1.1 copy-start.2
  1.9 1.1 copy-start.3
  1.9 1.1 copy-start.4
  1.9 1.1 copy-start.5
  1.9 1.1 copy-start.6
  1.9 1.1 copy-start.7

commit v6 on v5

--- a/solution.py
+++ b/solution.py
@@ -125,13 +125,17 @@
     def arrived(kind, t):
         arrival(targets[kind].at[t], m_r.at[kind, t], (dp, t))
 
-    def give_all(kind):
-        def one(k, carry):
-            message(kind, after(k)).start()
-            return carry
-
-        lax.fori_loop(1, SEQ, one, 0)
-        keep(kind)
+    def give_group(kind, core):
+        for n in range(TEAM):
+            t = core * TEAM + n
+
+            @pl.when(t != r)
+            def _():
+                message(kind, t).start()
+
+            @pl.when(t == r)
+            def _():
+                keep(kind)
 
     def got_all(kind):
         def one(k, carry):
@@ -284,13 +288,13 @@
             i = core * XS + n
             stage_qk[2 * i] = merge(q, k)
             stage_qk[2 * i + 1] = merge_high(q, k)
-    give_all(0)
+        give_group(0, core)
 
     forward_x(cot8, cot_s, cot_r, cot_h)
     from_all_y(v_part, v_r)
     for core in (c, 1 - c):
         packed(stage_v, core, dot(group_rows(hid8, core), wg[:, 256:384]).astype(BF))
-    give_all(1)
+        give_group(1, core)
     from_all_y(out_part, o_r)
     for j in range(TEAM):
         block = wg[128 * j : 128 * j + 128, 384:512]
@@ -302,8 +306,8 @@
         if core is not c:
             other_core(cot8, cot_r)
         packed(stage_g, core, dot(group_rows(cot8, core), wo[...]).astype(BF))
-
-    give_all(2)
+        give_group(2, core)
+
 
     for n in range(3):
         w_t[128 * n : 128 * n + 128, :] = wg[:, 128 * n : 128 * n + 128].T

time: 117 us -> 116 us (level); the launches traced: 117 us -> 113 us
  Pallas kernels: 111 us -> 108 us
    pallas_call x1, Pallas kernels: 111 us -> 108 us  [layer(): pl.pallas_call(kernel, out_shape=[jax.ShapeDtypeStruct(act, BF), jax.Shap...]
where the time goes in v6:
time: 116 us; the launch traced here: 113 us
  Pallas kernels  108 us (93%)
  local copies, waits for them, and re-layouts  4.69 us (4%)
    pallas_call x1, Pallas kernels, layer(): pl.pallas_call(kernel, out_shape=[jax.ShapeDtypeStruct(act, BF), jax.Shap...  108 us
    unnamed x19, local copies, waits for them, and re-layouts  4.31 us

profile of v6, /device:TPU:1, one launch (start us, length us, event | category | flops | bytes accessed | tf_op | source)
XLA Modules:
  0.0 113.4 jit_solution(10754090408315950961)
XLA Ops:
  0.6 0.0 copy-start
  0.6 1.0 copy-done
  1.7 0.2 bitcast_bitcast_fusion
  1.9 0.0 copy-start.1
  1.9 0.0 copy-start.2
  1.9 0.0 copy-start.3
  1.9 0.0 copy-start.4
  1.9 0.0 copy-start.5
  1.9 0.0 copy-start.6
  1.9 0.0 copy-start.7
  1.9 0.2 reshape.13.wt
  2.2 0.7 copy-done.1
  2.9 0.1 copy-done.2
  2.9 0.1 copy-done.3
  3.0 0.0 copy-done.4
  3.0 0.0 copy-done.5
  3.0 0.0 copy-done.6
  3.0 0.0 copy-done.7
  3.0 108.0 %shard_map.103 = (bf16[128,1024]{1,0:T(8,128)(2,1)S(1)}, bf16[128,1024]{1,0:T(8,128)(2,1)S(1)}, f32[64,4,1024]{2,1,0:T(4,128)S(1)}) custom-call(bf16[128,1024]{1,0:T(8,128)(2,1)S(1)} %bitcast.16, s32[1,128]{1,0:T(1,128)S(1)} %copy-done.5, bf16[173,1024]{1,0:T(8,128)(2,1)S(1)} %copy-done.1, s32[1,16]{1,0:T(1,128)S(1)} %copy-done.6, s32[4,16]{1,0:T(4,128)S(1)} %bitcast.18, ...), custom_call_target="tpu_custom_call" | custom-call | tf_op jit(solution)/shard_map/pallas_call | solution.py:662
  111.0 0.7 copy.17
  111.7 0.7 copy.18
  112.4 1.0 copy.19
Async XLA Ops:
  0.6 1.0 copy-start
  1.9 1.0 copy-start.1
  1.9 1.1 copy-start.2
  1.9 1.1 copy-start.3
  1.9 1.1 copy-start.4
  1.9 1.1 copy-start.5
  1.9 1.1 copy-start.6
  1.9 1.1 copy-start.7
